TPU v7x, 32 devices: a whole 2x2x4 slice. The times are simulated.
32 devices in a mesh: groups: 2 (over x), blk: 16 (over z, y, core).
Axes of the slice: x: 2, y: 2, z: 4, core: 2. Of those that a mesh axis runs over, the one named last changes fastest.
Arguments:
- queries: bfloat16 [4096, 512], P(('groups', 'blk')), parts along dimension 0, may hold values from -8 to 8
- key_states: bfloat16 [4096, 128], P(('groups', 'blk')), parts along dimension 0, may hold values from -6 to 6
- value_states: bfloat16 [4096, 128], P(('groups', 'blk')), parts along dimension 0, may hold values from -6 to 6
- grad_out: bfloat16 [4096, 512], P(('groups', 'blk')), parts along dimension 0, may hold values from -6 to 6
- tile_mask: int32 [32, 16], P('groups'), parts along dimension 0, may hold values 0 or 1
- block_order: int32 [32], P('groups'), parts along dimension 0, may hold values from 0 to 15, each once
Outputs:
- attended: bfloat16 [4096, 512], P(('groups', 'blk')), parts along dimension 0
- grad_queries: bfloat16 [4096, 512], P(('groups', 'blk')), parts along dimension 0
- grad_keys: float32 [4096, 128], P(('groups', 'blk')), parts along dimension 0
- grad_values: float32 [4096, 128], P(('groups', 'blk')), parts along dimension 0
There are 2 independent parts, one for each index of `groups`. A program takes and returns all parts, laid end to end along the dimension named above; each array names one. Nothing has to cross between parts.
Inputs may be any that keep to these rules, and one draw needn't show every extreme that they name: `block_order`: each block number appears once.
All inputs are finite; a program needn't handle non-finite values.
Results may differ from a plain program's by a relative error of at most 0.04.
Values may be sent and summed in bfloat16 or wider, within the bound.
A program may use at most 64 MiB of HBM per device.

v0:
```python
import jax
import jax.numpy as jnp
from jax import lax
from jax.sharding import PartitionSpec as P

TILE = 128


def passed_along(value, axis, steps):
    count = lax.axis_size(axis)
    pairs = [(source, (source + steps) % count) for source in range(count)]
    return lax.ppermute(value, axis, pairs)


def shards(queries, key_states, value_states, grad_out, tile_mask, block_order):
    cycle_size = lax.axis_size("blk")
    my_index = lax.axis_index("blk")
    tok_rows = key_states.shape[0]
    head_width = key_states.shape[1]
    head_count = queries.shape[1] // head_width
    scaling = head_width ** (-0.5)
    tiles_per = tok_rows // TILE
    tile_total = tile_mask.shape[1]
    offsets = jnp.arange(tok_rows, dtype=jnp.int32)
    my_block = block_order[my_index]
    total_rows = head_count * tok_rows

    def to_rows(features):
        return (
            features.reshape(tok_rows, head_count, head_width)
            .transpose(1, 0, 2)
            .reshape(total_rows, head_width)
        )

    def from_rows(row_form):
        return (
            row_form.reshape(head_count, tok_rows, head_width)
            .transpose(1, 0, 2)
            .reshape(tok_rows, head_count * head_width)
        )

    query_rows = to_rows(queries)
    cot_rows = to_rows(grad_out)

    def mask_for(query_block, key_pos):
        query_pos = query_block * tok_rows + offsets
        tile_rows = lax.dynamic_slice_in_dim(
            tile_mask, query_block * tiles_per, tiles_per, 0
        ).astype(jnp.float32)
        tile_rows = jnp.repeat(tile_rows, TILE, axis=0)
        one_hot = (
            (key_pos // TILE)[:, None] == jnp.arange(tile_total, dtype=jnp.int32)[None, :]
        ).astype(jnp.float32)
        tile_bits = jnp.dot(tile_rows, one_hot.T, preferred_element_type=jnp.float32) > 0.5
        same_tile = (query_pos // TILE)[:, None] == (key_pos // TILE)[None, :]
        allowed = (query_pos[:, None] >= key_pos[None, :]) & (tile_bits | same_tile)
        return jnp.tile(allowed, (head_count, 1))

    def softmax_update(carry_state, key_sub, value_sub, allowed):
        run_max, run_sum, run_acc = carry_state
        scores = (
            jnp.einsum("rd,kd->rk", query_rows, key_sub, preferred_element_type=jnp.float32)
            * scaling
        )
        scores = jnp.where(allowed, scores, -1e30)
        new_max = jnp.maximum(run_max, jnp.max(scores, axis=1))
        weights = jnp.where(allowed, jnp.exp(scores - new_max[:, None]), 0.0)
        factor = jnp.exp(run_max - new_max)
        run_sum = run_sum * factor + jnp.sum(weights, axis=1)
        run_acc = run_acc * factor[:, None] + jnp.dot(
            weights.astype(jnp.bfloat16), value_sub, preferred_element_type=jnp.float32
        )
        return (new_max, run_sum, run_acc)

    def guarded_update(carry_state, key_sub, value_sub, allowed):
        return softmax_update(carry_state, key_sub, value_sub, allowed)

    start_state = (
        jnp.full((total_rows,), -1e30, jnp.float32),
        jnp.zeros((total_rows,), jnp.float32),
        jnp.zeros((total_rows, head_width), jnp.float32),
    )
    key_piece = lax.all_gather(key_states, "blk", axis=0, tiled=True)
    value_piece = lax.all_gather(value_states, "blk", axis=0, tiled=True)
    piece_rows = key_piece.shape[0]

    def sub_step(sub_num, inner_state):
        first = sub_num * tok_rows
        key_sub = lax.dynamic_slice_in_dim(key_piece, first, tok_rows, 0)
        value_sub = lax.dynamic_slice_in_dim(value_piece, first, tok_rows, 0)
        key_ids = first + jnp.arange(tok_rows, dtype=jnp.int32)
        owners = key_ids // tok_rows
        owner_blocks = jnp.sum(
            jnp.where(
                owners[:, None] == jnp.arange(cycle_size, dtype=jnp.int32)[None, :],
                block_order[None, :],
                0,
            ),
            axis=1,
        )
        key_pos = owner_blocks * tok_rows + key_ids % tok_rows
        return guarded_update(inner_state, key_sub, value_sub, mask_for(my_block, key_pos))

    run_max, run_sum, run_acc = lax.fori_loop(0, piece_rows // tok_rows, sub_step, start_state)
    log_sum = run_max + jnp.log(run_sum)
    out_rows = (run_acc / run_sum[:, None]).astype(jnp.bfloat16)
    attended = from_rows(out_rows)
    row_delta = jnp.sum(cot_rows.astype(jnp.float32) * out_rows.astype(jnp.float32), axis=1)

    def block_grads(q_part, cot_part, sum_part, delta_part, key_sub, value_sub, allowed):
        scores = (
            jnp.einsum("rd,kd->rk", q_part, key_sub, preferred_element_type=jnp.float32) * scaling
        )
        weights = jnp.where(allowed, jnp.exp(scores - sum_part[:, None]), 0.0)
        value_term = jnp.einsum(
            "rk,rd->kd", weights.astype(jnp.bfloat16), cot_part, preferred_element_type=jnp.float32
        )
        d_prob = jnp.einsum("rd,kd->rk", cot_part, value_sub, preferred_element_type=jnp.float32)
        d_score = (weights * (d_prob - delta_part[:, None])).astype(jnp.bfloat16)
        query_term = jnp.dot(d_score, key_sub, preferred_element_type=jnp.float32) * scaling
        key_term = (
            jnp.einsum("rk,rd->kd", d_score, q_part, preferred_element_type=jnp.float32) * scaling
        )
        return (query_term, key_term, value_term)

    def guarded_grads(q_part, cot_part, sum_part, delta_part, key_sub, value_sub, allowed):
        return block_grads(q_part, cot_part, sum_part, delta_part, key_sub, value_sub, allowed)

    zero_keys = jnp.zeros((tok_rows, head_width), jnp.float32)
    zero_queries = jnp.zeros((total_rows, head_width), jnp.float32)

    def key_step(step_num, carry_state):
        key_cur, value_cur, key_acc, value_acc, query_acc = carry_state
        source = (my_index - step_num) % cycle_size
        key_pos = block_order[source] * tok_rows + offsets
        allowed = mask_for(my_block, key_pos)
        query_term, key_term, value_term = guarded_grads(
            query_rows, cot_rows, log_sum, row_delta, key_cur, value_cur, allowed
        )
        return (
            key_cur,
            value_cur,
            key_acc + key_term,
            value_acc + value_term,
            query_acc + query_term,
        )

    def key_turn(step_num, carry_state):
        key_cur, value_cur, key_acc, value_acc, query_acc = key_step(step_num, carry_state)
        key_cur, value_cur = passed_along((key_cur, value_cur), "blk", 1)
        key_acc, value_acc = passed_along((key_acc, value_acc), "blk", 1)
        return (key_cur, value_cur, key_acc, value_acc, query_acc)

    carry_state = (key_states, value_states, zero_keys, zero_keys, zero_queries)
    carry_state = lax.fori_loop(0, cycle_size - 1, key_turn, carry_state)
    carry_state = key_step(cycle_size - 1, carry_state)
    key_acc, value_acc = passed_along((carry_state[2], carry_state[3]), "blk", 1)
    query_acc = carry_state[4]
    grad_queries = from_rows(query_acc.astype(jnp.bfloat16))
    return (attended, grad_queries, key_acc, value_acc)


def solution(mesh):
    placed = (
        P(("groups", "blk"), None),
        P(("groups", "blk"), None),
        P(("groups", "blk"), None),
        P(("groups", "blk"), None),
        P("groups", None),
        P("groups"),
    )
    return jax.shard_map(
        shards,
        mesh=mesh,
        in_specs=placed,
        out_specs=(
            P(("groups", "blk"), None),
            P(("groups", "blk"), None),
            P(("groups", "blk"), None),
            P(("groups", "blk"), None),
        ),
        check_vma=False,
    )
```

profile of v0, /device:TPU:0, one launch (start us, length us, event | category | flops | bytes accessed | tf_op | source)
XLA Modules:
  0.0 222.9 jit_solution(3966216597943441637)
XLA Ops:
  0.7 0.8 copy.83
  1.5 0.7 copy-done.3
  4.7 0.7 dynamic-slice_convert_fusion
  5.4 0.7 fusion.73
  6.8 24.6 %all_gather.6 = bf16[2048,128]{1,0:T(8,128)(2,1)S(1)} all-gather(bf16[128,128]{1,0:T(8,128)(2,1)S(1)} %copy.83), channel_id=1, replica_groups=mesh['groups'=2,'blk'=16] {'blk'}, dimensions={0}, use_global_device_ids=true | all-gather | bytes 557056 | tf_op jit(solution)/shard_map/all_gather | solution.py:83
  31.4 18.9 %all_gather.7 = bf16[2048,128]{1,0:T(8,128)(2,1)S(1)} all-gather(bf16[128,128]{1,0:T(8,128)(2,1)S(1)} %copy.84), channel_id=1, replica_groups=mesh['groups'=2,'blk'=16] {'blk'}, dimensions={0}, use_global_device_ids=true | all-gather | bytes 557056 | tf_op jit(solution)/shard_map/all_gather | solution.py:84
  50.2 17.7 %while.47 = (s32[]{:T(128)}, f32[512]{0:T(512)S(1)}, f32[512]{0:T(512)S(1)}, f32[512,128]{1,0:T(8,128)S(1)}, s32[]{:T(128)}, /*index=5*/s32[16]{0:T(128)S(1)}, b...) while((s32[]{:T(128)}, f32[512]{0:T(512)S(1)}, ...), condition=%wide.region_4.5_spmd.clone, body=%wide.region_0.4_spmd.clone.sunk | while | flops 34965508 | bytes 1841459 | solution.py:104
  69.2 144.8 %while.48 = (s32[]{:T(128)}, bf16[128,128]{1,0:T(8,128)(2,1)S(1)}, bf16[128,128]{1,0:T(8,128)(2,1)S(1)}, f32[128,128]{1,0:T(8,128)S(1)}, f32[128,128]{1,0:T(8,12...) while((s32[]{:T(128)}, bf16[128,128]{1,0:T(8,128)(2,1)S(1)}, ...), condition=%wide.region_7.8_spmd.clone.clone, body=%wide.region_6.7_spmd.clone.clone.sunk | while | flops 85202960 | bytes 3711538 | solution.py:155
  69.7 1.5 collective-permute-start.1
  74.4 0.9 collective-permute-done
  75.7 4.2 %collective-permute-done.2 = f32[128,128]{1,0:T(8,128)S(1)} collective-permute-done((f32[128,128]{1,0:T(8,128)S(1)}, f32[128,128]{1,0:T(8,128)S(1)}, u32[]{:S(2)}, u32[]{:S(2)}) %collective-permute-start.2) | collective-permute-done | bytes 65568 | tf_op jit(solution)/shard_map/while/body/eval_jaxpr/ppermute | solution.py:12
  79.9 0.7 collective-permute-done.3
  80.7 0.6 dynamic_slice.79
  83.6 3.1 %collective-permute-done = bf16[128,128]{1,0:T(8,128)(2,1)S(1)} collective-permute-done((bf16[128,128]{1,0:T(8,128)(2,1)S(1)}, bf16[128,128]{1,0:T(8,128)(2,1)S(1)}, u32[]{:S(2)}, u32[]{:S(2)}) %collective-permute-start) | collective-permute-done | bytes 32800 | tf_op jit(solution)/shard_map/while/body/eval_jaxpr/ppermute | solution.py:12
  87.0 2.4 %collective-permute-done.2 = f32[128,128]{1,0:T(8,128)S(1)} collective-permute-done((f32[128,128]{1,0:T(8,128)S(1)}, f32[128,128]{1,0:T(8,128)S(1)}, u32[]{:S(2)}, u32[]{:S(2)}) %collective-permute-start.2) | collective-permute-done | bytes 65568 | tf_op jit(solution)/shard_map/while/body/eval_jaxpr/ppermute | solution.py:12
  89.4 0.7 collective-permute-done.3
  90.2 0.6 dynamic_slice.79
  93.1 3.1 %collective-permute-done = bf16[128,128]{1,0:T(8,128)(2,1)S(1)} collective-permute-done((bf16[128,128]{1,0:T(8,128)(2,1)S(1)}, bf16[128,128]{1,0:T(8,128)(2,1)S(1)}, u32[]{:S(2)}, u32[]{:S(2)}) %collective-permute-start) | collective-permute-done | bytes 32800 | tf_op jit(solution)/shard_map/while/body/eval_jaxpr/ppermute | solution.py:12
  96.5 2.4 %collective-permute-done.2 = f32[128,128]{1,0:T(8,128)S(1)} collective-permute-done((f32[128,128]{1,0:T(8,128)S(1)}, f32[128,128]{1,0:T(8,128)S(1)}, u32[]{:S(2)}, u32[]{:S(2)}) %collective-permute-start.2) | collective-permute-done | bytes 65568 | tf_op jit(solution)/shard_map/while/body/eval_jaxpr/ppermute | solution.py:12
  98.9 0.7 collective-permute-done.3
  102.6 3.1 %collective-permute-done = bf16[128,128]{1,0:T(8,128)(2,1)S(1)} collective-permute-done((bf16[128,128]{1,0:T(8,128)(2,1)S(1)}, bf16[128,128]{1,0:T(8,128)(2,1)S(1)}, u32[]{:S(2)}, u32[]{:S(2)}) %collective-permute-start) | collective-permute-done | bytes 32800 | tf_op jit(solution)/shard_map/while/body/eval_jaxpr/ppermute | solution.py:12
  106.0 2.4 %collective-permute-done.2 = f32[128,128]{1,0:T(8,128)S(1)} collective-permute-done((f32[128,128]{1,0:T(8,128)S(1)}, f32[128,128]{1,0:T(8,128)S(1)}, u32[]{:S(2)}, u32[]{:S(2)}) %collective-permute-start.2) | collective-permute-done | bytes 65568 | tf_op jit(solution)/shard_map/while/body/eval_jaxpr/ppermute | solution.py:12
  108.5 0.7 collective-permute-done.3
  109.3 0.6 dynamic_slice.79
  112.2 3.1 %collective-permute-done = bf16[128,128]{1,0:T(8,128)(2,1)S(1)} collective-permute-done((bf16[128,128]{1,0:T(8,128)(2,1)S(1)}, bf16[128,128]{1,0:T(8,128)(2,1)S(1)}, u32[]{:S(2)}, u32[]{:S(2)}) %collective-permute-start) | collective-permute-done | bytes 32800 | tf_op jit(solution)/shard_map/while/body/eval_jaxpr/ppermute | solution.py:12
  115.6 2.4 %collective-permute-done.2 = f32[128,128]{1,0:T(8,128)S(1)} collective-permute-done((f32[128,128]{1,0:T(8,128)S(1)}, f32[128,128]{1,0:T(8,128)S(1)}, u32[]{:S(2)}, u32[]{:S(2)}) %collective-permute-start.2) | collective-permute-done | bytes 65568 | tf_op jit(solution)/shard_map/while/body/eval_jaxpr/ppermute | solution.py:12
  118.0 0.7 collective-permute-done.3
  121.7 3.1 %collective-permute-done = bf16[128,128]{1,0:T(8,128)(2,1)S(1)} collective-permute-done((bf16[128,128]{1,0:T(8,128)(2,1)S(1)}, bf16[128,128]{1,0:T(8,128)(2,1)S(1)}, u32[]{:S(2)}, u32[]{:S(2)}) %collective-permute-start) | collective-permute-done | bytes 32800 | tf_op jit(solution)/shard_map/while/body/eval_jaxpr/ppermute | solution.py:12
  125.1 2.4 %collective-permute-done.2 = f32[128,128]{1,0:T(8,128)S(1)} collective-permute-done((f32[128,128]{1,0:T(8,128)S(1)}, f32[128,128]{1,0:T(8,128)S(1)}, u32[]{:S(2)}, u32[]{:S(2)}) %collective-permute-start.2) | collective-permute-done | bytes 65568 | tf_op jit(solution)/shard_map/while/body/eval_jaxpr/ppermute | solution.py:12
  127.5 0.7 collective-permute-done.3
  131.2 3.1 %collective-permute-done = bf16[128,128]{1,0:T(8,128)(2,1)S(1)} collective-permute-done((bf16[128,128]{1,0:T(8,128)(2,1)S(1)}, bf16[128,128]{1,0:T(8,128)(2,1)S(1)}, u32[]{:S(2)}, u32[]{:S(2)}) %collective-permute-start) | collective-permute-done | bytes 32800 | tf_op jit(solution)/shard_map/while/body/eval_jaxpr/ppermute | solution.py:12
  134.6 2.4 %collective-permute-done.2 = f32[128,128]{1,0:T(8,128)S(1)} collective-permute-done((f32[128,128]{1,0:T(8,128)S(1)}, f32[128,128]{1,0:T(8,128)S(1)}, u32[]{:S(2)}, u32[]{:S(2)}) %collective-permute-start.2) | collective-permute-done | bytes 65568 | tf_op jit(solution)/shard_map/while/body/eval_jaxpr/ppermute | solution.py:12
  137.1 0.7 collective-permute-done.3
  140.8 3.1 %collective-permute-done = bf16[128,128]{1,0:T(8,128)(2,1)S(1)} collective-permute-done((bf16[128,128]{1,0:T(8,128)(2,1)S(1)}, bf16[128,128]{1,0:T(8,128)(2,1)S(1)}, u32[]{:S(2)}, u32[]{:S(2)}) %collective-permute-start) | collective-permute-done | bytes 32800 | tf_op jit(solution)/shard_map/while/body/eval_jaxpr/ppermute | solution.py:12
  144.2 2.4 %collective-permute-done.2 = f32[128,128]{1,0:T(8,128)S(1)} collective-permute-done((f32[128,128]{1,0:T(8,128)S(1)}, f32[128,128]{1,0:T(8,128)S(1)}, u32[]{:S(2)}, u32[]{:S(2)}) %collective-permute-start.2) | collective-permute-done | bytes 65568 | tf_op jit(solution)/shard_map/while/body/eval_jaxpr/ppermute | solution.py:12
  146.6 0.7 collective-permute-done.3
  150.3 3.1 %collective-permute-done = bf16[128,128]{1,0:T(8,128)(2,1)S(1)} collective-permute-done((bf16[128,128]{1,0:T(8,128)(2,1)S(1)}, bf16[128,128]{1,0:T(8,128)(2,1)S(1)}, u32[]{:S(2)}, u32[]{:S(2)}) %collective-permute-start) | collective-permute-done | bytes 32800 | tf_op jit(solution)/shard_map/while/body/eval_jaxpr/ppermute | solution.py:12
  153.7 2.4 %collective-permute-done.2 = f32[128,128]{1,0:T(8,128)S(1)} collective-permute-done((f32[128,128]{1,0:T(8,128)S(1)}, f32[128,128]{1,0:T(8,128)S(1)}, u32[]{:S(2)}, u32[]{:S(2)}) %collective-permute-start.2) | collective-permute-done | bytes 65568 | tf_op jit(solution)/shard_map/while/body/eval_jaxpr/ppermute | solution.py:12
  156.1 0.7 collective-permute-done.3
  159.8 3.1 %collective-permute-done = bf16[128,128]{1,0:T(8,128)(2,1)S(1)} collective-permute-done((bf16[128,128]{1,0:T(8,128)(2,1)S(1)}, bf16[128,128]{1,0:T(8,128)(2,1)S(1)}, u32[]{:S(2)}, u32[]{:S(2)}) %collective-permute-start) | collective-permute-done | bytes 32800 | tf_op jit(solution)/shard_map/while/body/eval_jaxpr/ppermute | solution.py:12
  163.2 2.4 %collective-permute-done.2 = f32[128,128]{1,0:T(8,128)S(1)} collective-permute-done((f32[128,128]{1,0:T(8,128)S(1)}, f32[128,128]{1,0:T(8,128)S(1)}, u32[]{:S(2)}, u32[]{:S(2)}) %collective-permute-start.2) | collective-permute-done | bytes 65568 | tf_op jit(solution)/shard_map/while/body/eval_jaxpr/ppermute | solution.py:12
  165.7 0.7 collective-permute-done.3
  169.4 3.1 %collective-permute-done = bf16[128,128]{1,0:T(8,128)(2,1)S(1)} collective-permute-done((bf16[128,128]{1,0:T(8,128)(2,1)S(1)}, bf16[128,128]{1,0:T(8,128)(2,1)S(1)}, u32[]{:S(2)}, u32[]{:S(2)}) %collective-permute-start) | collective-permute-done | bytes 32800 | tf_op jit(solution)/shard_map/while/body/eval_jaxpr/ppermute | solution.py:12
  172.8 2.4 %collective-permute-done.2 = f32[128,128]{1,0:T(8,128)S(1)} collective-permute-done((f32[128,128]{1,0:T(8,128)S(1)}, f32[128,128]{1,0:T(8,128)S(1)}, u32[]{:S(2)}, u32[]{:S(2)}) %collective-permute-start.2) | collective-permute-done | bytes 65568 | tf_op jit(solution)/shard_map/while/body/eval_jaxpr/ppermute | solution.py:12
  175.2 0.7 collective-permute-done.3
  176.0 0.6 dynamic_slice.79
  178.9 3.1 %collective-permute-done = bf16[128,128]{1,0:T(8,128)(2,1)S(1)} collective-permute-done((bf16[128,128]{1,0:T(8,128)(2,1)S(1)}, bf16[128,128]{1,0:T(8,128)(2,1)S(1)}, u32[]{:S(2)}, u32[]{:S(2)}) %collective-permute-start) | collective-permute-done | bytes 32800 | tf_op jit(solution)/shard_map/while/body/eval_jaxpr/ppermute | solution.py:12
  182.3 2.4 %collective-permute-done.2 = f32[128,128]{1,0:T(8,128)S(1)} collective-permute-done((f32[128,128]{1,0:T(8,128)S(1)}, f32[128,128]{1,0:T(8,128)S(1)}, u32[]{:S(2)}, u32[]{:S(2)}) %collective-permute-start.2) | collective-permute-done | bytes 65568 | tf_op jit(solution)/shard_map/while/body/eval_jaxpr/ppermute | solution.py:12
  184.7 0.7 collective-permute-done.3
  188.4 3.1 %collective-permute-done = bf16[128,128]{1,0:T(8,128)(2,1)S(1)} collective-permute-done((bf16[128,128]{1,0:T(8,128)(2,1)S(1)}, bf16[128,128]{1,0:T(8,128)(2,1)S(1)}, u32[]{:S(2)}, u32[]{:S(2)}) %collective-permute-start) | collective-permute-done | bytes 32800 | tf_op jit(solution)/shard_map/while/body/eval_jaxpr/ppermute | solution.py:12
  191.8 2.4 %collective-permute-done.2 = f32[128,128]{1,0:T(8,128)S(1)} collective-permute-done((f32[128,128]{1,0:T(8,128)S(1)}, f32[128,128]{1,0:T(8,128)S(1)}, u32[]{:S(2)}, u32[]{:S(2)}) %collective-permute-start.2) | collective-permute-done | bytes 65568 | tf_op jit(solution)/shard_map/while/body/eval_jaxpr/ppermute | solution.py:12
  194.3 0.7 collective-permute-done.3
  197.9 3.1 %collective-permute-done = bf16[128,128]{1,0:T(8,128)(2,1)S(1)} collective-permute-done((bf16[128,128]{1,0:T(8,128)(2,1)S(1)}, bf16[128,128]{1,0:T(8,128)(2,1)S(1)}, u32[]{:S(2)}, u32[]{:S(2)}) %collective-permute-start) | collective-permute-done | bytes 32800 | tf_op jit(solution)/shard_map/while/body/eval_jaxpr/ppermute | solution.py:12
  201.4 2.4 %collective-permute-done.2 = f32[128,128]{1,0:T(8,128)S(1)} collective-permute-done((f32[128,128]{1,0:T(8,128)S(1)}, f32[128,128]{1,0:T(8,128)S(1)}, u32[]{:S(2)}, u32[]{:S(2)}) %collective-permute-start.2) | collective-permute-done | bytes 65568 | tf_op jit(solution)/shard_map/while/body/eval_jaxpr/ppermute | solution.py:12
  203.8 0.7 collective-permute-done.3
  207.5 3.1 %collective-permute-done = bf16[128,128]{1,0:T(8,128)(2,1)S(1)} collective-permute-done((bf16[128,128]{1,0:T(8,128)(2,1)S(1)}, bf16[128,128]{1,0:T(8,128)(2,1)S(1)}, u32[]{:S(2)}, u32[]{:S(2)}) %collective-permute-start) | collective-permute-done | bytes 32800 | tf_op jit(solution)/shard_map/while/body/eval_jaxpr/ppermute | solution.py:12
  210.9 2.4 %collective-permute-done.2 = f32[128,128]{1,0:T(8,128)S(1)} collective-permute-done((f32[128,128]{1,0:T(8,128)S(1)}, f32[128,128]{1,0:T(8,128)S(1)}, u32[]{:S(2)}, u32[]{:S(2)}) %collective-permute-start.2) | collective-permute-done | bytes 65568 | tf_op jit(solution)/shard_map/while/body/eval_jaxpr/ppermute | solution.py:12
  213.3 0.7 collective-permute-done.3
  215.2 0.7 copy.41
  216.0 0.7 copy.40
  216.7 4.2 %collective-permute-done.5 = f32[128,128]{1,0:T(8,128)S(1)} collective-permute-done((f32[128,128]{1,0:T(8,128)S(1)}, f32[128,128]{1,0:T(8,128)S(1)}, u32[]{:S(2)}, u32[]{:S(2)}) %collective-permute-start.5) | collective-permute-done | bytes 65568 | tf_op jit(solution)/shard_map/ppermute | solution.py:12
  220.9 0.7 collective-permute-done.4
  221.7 0.6 copy.85
  222.3 0.6 copy.86
  (489 shorter events, 55.5 us)
Async XLA Ops:
  0.6 6.1 %copy-start = (bf16[128,512]{1,0:T(8,128)(2,1)S(1)}, bf16[128,512]{1,0:T(8,128)(2,1)}, u32[]{:S(2)}) copy-start(bf16[128,512]{1,0:T(8,128)(2,1)} %param.10) | copy-start | bytes 393220
  50.2 17.7 %copy-start.1 = (bf16[128,512]{1,0:T(8,128)(2,1)S(1)}, bf16[128,512]{1,0:T(8,128)(2,1)}, u32[]{:S(2)}) copy-start(bf16[128,512]{1,0:T(8,128)(2,1)} %param.13) | copy-start | bytes 393220
  69.3 6.1 %collective-permute-start = (bf16[128,128]{1,0:T(8,128)(2,1)S(1)}, bf16[128,128]{1,0:T(8,128)(2,1)S(1)}, u32[]{:S(2)}, u32[]{:S(2)}) collective-permute-start(bf16[128,128]{1,0:T(8,128)(2,1)S(1)} %copy.67), channel_id=1, source_target_pairs={{0,1},{1,2},{2,3},{3,4},{4,5},{5,6},{6,7},{7,8},{8,9},{9,10},{10,1... | collective-permute-start | bytes 98312 | tf_op jit(solution)/shard_map/while/body/eval_jaxpr/ppermute | solution.py:12
  69.7 6.0 %collective-permute-start.1 = (bf16[128,128]{1,0:T(8,128)(2,1)S(1)}, bf16[128,128]{1,0:T(8,128)(2,1)S(1)}, u32[]{:S(2)}, u32[]{:S(2)}) collective-permute-start(bf16[128,128]{1,0:T(8,128)(2,1)S(1)} %copy.68), channel_id=1, source_target_pairs={{0,1},{1,2},{2,3},{3,4},{4,5},{5,6},{6,7},{7,8},{8,9},{9,10},{10,1... | collective-permute-start | bytes 98312 | tf_op jit(solution)/shard_map/while/body/eval_jaxpr/ppermute | solution.py:12
  73.4 6.4 %collective-permute-start.2 = (f32[128,128]{1,0:T(8,128)S(1)}, f32[128,128]{1,0:T(8,128)S(1)}, u32[]{:S(2)}, u32[]{:S(2)}) collective-permute-start(f32[128,128]{1,0:T(8,128)S(1)} %fusion.122), channel_id=1, source_target_pairs={{0,1},{1,2},{2,3},{3,4},{4,5},{5,6},{6,7},{7,8},{8,9},{9,10},{10,1... | collective-permute-start | bytes 196616 | tf_op jit(solution)/shard_map/while/body/eval_jaxpr/ppermute | solution.py:12
  74.1 6.5 %collective-permute-start.3 = (f32[128,128]{1,0:T(8,128)S(1)}, f32[128,128]{1,0:T(8,128)S(1)}, u32[]{:S(2)}, u32[]{:S(2)}) collective-permute-start(f32[128,128]{1,0:T(8,128)S(1)} %convolution_add_fusion.6), channel_id=1, source_target_pairs={{0,1},{1,2},{2,3},{3,4},{4,5},{5,6},{6,7},{7,8},{8,9},{9,10},{10,1... | collective-permute-start | bytes 196616 | tf_op jit(solution)/shard_map/while/body/eval_jaxpr/ppermute | solution.py:12
  80.6 6.0 %collective-permute-start = (bf16[128,128]{1,0:T(8,128)(2,1)S(1)}, bf16[128,128]{1,0:T(8,128)(2,1)S(1)}, u32[]{:S(2)}, u32[]{:S(2)}) collective-permute-start(bf16[128,128]{1,0:T(8,128)(2,1)S(1)} %copy.67), channel_id=1, source_target_pairs={{0,1},{1,2},{2,3},{3,4},{4,5},{5,6},{6,7},{7,8},{8,9},{9,10},{10,1... | collective-permute-start | bytes 98312 | tf_op jit(solution)/shard_map/while/body/eval_jaxpr/ppermute | solution.py:12
  80.6 6.4 %collective-permute-start.1 = (bf16[128,128]{1,0:T(8,128)(2,1)S(1)}, bf16[128,128]{1,0:T(8,128)(2,1)S(1)}, u32[]{:S(2)}, u32[]{:S(2)}) collective-permute-start(bf16[128,128]{1,0:T(8,128)(2,1)S(1)} %copy.68), channel_id=1, source_target_pairs={{0,1},{1,2},{2,3},{3,4},{4,5},{5,6},{6,7},{7,8},{8,9},{9,10},{10,1... | collective-permute-start | bytes 98312 | tf_op jit(solution)/shard_map/while/body/eval_jaxpr/ppermute | solution.py:12
  83.0 6.4 %collective-permute-start.2 = (f32[128,128]{1,0:T(8,128)S(1)}, f32[128,128]{1,0:T(8,128)S(1)}, u32[]{:S(2)}, u32[]{:S(2)}) collective-permute-start(f32[128,128]{1,0:T(8,128)S(1)} %fusion.122), channel_id=1, source_target_pairs={{0,1},{1,2},{2,3},{3,4},{4,5},{5,6},{6,7},{7,8},{8,9},{9,10},{10,1... | collective-permute-start | bytes 196616 | tf_op jit(solution)/shard_map/while/body/eval_jaxpr/ppermute | solution.py:12
  83.3 6.8 %collective-permute-start.3 = (f32[128,128]{1,0:T(8,128)S(1)}, f32[128,128]{1,0:T(8,128)S(1)}, u32[]{:S(2)}, u32[]{:S(2)}) collective-permute-start(f32[128,128]{1,0:T(8,128)S(1)} %convolution_add_fusion.6), channel_id=1, source_target_pairs={{0,1},{1,2},{2,3},{3,4},{4,5},{5,6},{6,7},{7,8},{8,9},{9,10},{10,1... | collective-permute-start | bytes 196616 | tf_op jit(solution)/shard_map/while/body/eval_jaxpr/ppermute | solution.py:12
  90.1 6.0 %collective-permute-start = (bf16[128,128]{1,0:T(8,128)(2,1)S(1)}, bf16[128,128]{1,0:T(8,128)(2,1)S(1)}, u32[]{:S(2)}, u32[]{:S(2)}) collective-permute-start(bf16[128,128]{1,0:T(8,128)(2,1)S(1)} %copy.67), channel_id=1, source_target_pairs={{0,1},{1,2},{2,3},{3,4},{4,5},{5,6},{6,7},{7,8},{8,9},{9,10},{10,1... | collective-permute-start | bytes 98312 | tf_op jit(solution)/shard_map/while/body/eval_jaxpr/ppermute | solution.py:12
  90.1 6.4 %collective-permute-start.1 = (bf16[128,128]{1,0:T(8,128)(2,1)S(1)}, bf16[128,128]{1,0:T(8,128)(2,1)S(1)}, u32[]{:S(2)}, u32[]{:S(2)}) collective-permute-start(bf16[128,128]{1,0:T(8,128)(2,1)S(1)} %copy.68), channel_id=1, source_target_pairs={{0,1},{1,2},{2,3},{3,4},{4,5},{5,6},{6,7},{7,8},{8,9},{9,10},{10,1... | collective-permute-start | bytes 98312 | tf_op jit(solution)/shard_map/while/body/eval_jaxpr/ppermute | solution.py:12
  92.5 6.4 %collective-permute-start.2 = (f32[128,128]{1,0:T(8,128)S(1)}, f32[128,128]{1,0:T(8,128)S(1)}, u32[]{:S(2)}, u32[]{:S(2)}) collective-permute-start(f32[128,128]{1,0:T(8,128)S(1)} %fusion.122), channel_id=1, source_target_pairs={{0,1},{1,2},{2,3},{3,4},{4,5},{5,6},{6,7},{7,8},{8,9},{9,10},{10,1... | collective-permute-start | bytes 196616 | tf_op jit(solution)/shard_map/while/body/eval_jaxpr/ppermute | solution.py:12
  92.8 6.8 %collective-permute-start.3 = (f32[128,128]{1,0:T(8,128)S(1)}, f32[128,128]{1,0:T(8,128)S(1)}, u32[]{:S(2)}, u32[]{:S(2)}) collective-permute-start(f32[128,128]{1,0:T(8,128)S(1)} %convolution_add_fusion.6), channel_id=1, source_target_pairs={{0,1},{1,2},{2,3},{3,4},{4,5},{5,6},{6,7},{7,8},{8,9},{9,10},{10,1... | collective-permute-start | bytes 196616 | tf_op jit(solution)/shard_map/while/body/eval_jaxpr/ppermute | solution.py:12
  99.6 6.0 %collective-permute-start = (bf16[128,128]{1,0:T(8,128)(2,1)S(1)}, bf16[128,128]{1,0:T(8,128)(2,1)S(1)}, u32[]{:S(2)}, u32[]{:S(2)}) collective-permute-start(bf16[128,128]{1,0:T(8,128)(2,1)S(1)} %copy.67), channel_id=1, source_target_pairs={{0,1},{1,2},{2,3},{3,4},{4,5},{5,6},{6,7},{7,8},{8,9},{9,10},{10,1... | collective-permute-start | bytes 98312 | tf_op jit(solution)/shard_map/while/body/eval_jaxpr/ppermute | solution.py:12
  99.7 6.4 %collective-permute-start.1 = (bf16[128,128]{1,0:T(8,128)(2,1)S(1)}, bf16[128,128]{1,0:T(8,128)(2,1)S(1)}, u32[]{:S(2)}, u32[]{:S(2)}) collective-permute-start(bf16[128,128]{1,0:T(8,128)(2,1)S(1)} %copy.68), channel_id=1, source_target_pairs={{0,1},{1,2},{2,3},{3,4},{4,5},{5,6},{6,7},{7,8},{8,9},{9,10},{10,1... | collective-permute-start | bytes 98312 | tf_op jit(solution)/shard_map/while/body/eval_jaxpr/ppermute | solution.py:12
  102.0 6.4 %collective-permute-start.2 = (f32[128,128]{1,0:T(8,128)S(1)}, f32[128,128]{1,0:T(8,128)S(1)}, u32[]{:S(2)}, u32[]{:S(2)}) collective-permute-start(f32[128,128]{1,0:T(8,128)S(1)} %fusion.122), channel_id=1, source_target_pairs={{0,1},{1,2},{2,3},{3,4},{4,5},{5,6},{6,7},{7,8},{8,9},{9,10},{10,1... | collective-permute-start | bytes 196616 | tf_op jit(solution)/shard_map/while/body/eval_jaxpr/ppermute | solution.py:12
  102.3 6.8 %collective-permute-start.3 = (f32[128,128]{1,0:T(8,128)S(1)}, f32[128,128]{1,0:T(8,128)S(1)}, u32[]{:S(2)}, u32[]{:S(2)}) collective-permute-start(f32[128,128]{1,0:T(8,128)S(1)} %convolution_add_fusion.6), channel_id=1, source_target_pairs={{0,1},{1,2},{2,3},{3,4},{4,5},{5,6},{6,7},{7,8},{8,9},{9,10},{10,1... | collective-permute-start | bytes 196616 | tf_op jit(solution)/shard_map/while/body/eval_jaxpr/ppermute | solution.py:12
  109.2 6.0 %collective-permute-start = (bf16[128,128]{1,0:T(8,128)(2,1)S(1)}, bf16[128,128]{1,0:T(8,128)(2,1)S(1)}, u32[]{:S(2)}, u32[]{:S(2)}) collective-permute-start(bf16[128,128]{1,0:T(8,128)(2,1)S(1)} %copy.67), channel_id=1, source_target_pairs={{0,1},{1,2},{2,3},{3,4},{4,5},{5,6},{6,7},{7,8},{8,9},{9,10},{10,1... | collective-permute-start | bytes 98312 | tf_op jit(solution)/shard_map/while/body/eval_jaxpr/ppermute | solution.py:12
  109.2 6.4 %collective-permute-start.1 = (bf16[128,128]{1,0:T(8,128)(2,1)S(1)}, bf16[128,128]{1,0:T(8,128)(2,1)S(1)}, u32[]{:S(2)}, u32[]{:S(2)}) collective-permute-start(bf16[128,128]{1,0:T(8,128)(2,1)S(1)} %copy.68), channel_id=1, source_target_pairs={{0,1},{1,2},{2,3},{3,4},{4,5},{5,6},{6,7},{7,8},{8,9},{9,10},{10,1... | collective-permute-start | bytes 98312 | tf_op jit(solution)/shard_map/while/body/eval_jaxpr/ppermute | solution.py:12
  111.6 6.4 %collective-permute-start.2 = (f32[128,128]{1,0:T(8,128)S(1)}, f32[128,128]{1,0:T(8,128)S(1)}, u32[]{:S(2)}, u32[]{:S(2)}) collective-permute-start(f32[128,128]{1,0:T(8,128)S(1)} %fusion.122), channel_id=1, source_target_pairs={{0,1},{1,2},{2,3},{3,4},{4,5},{5,6},{6,7},{7,8},{8,9},{9,10},{10,1... | collective-permute-start | bytes 196616 | tf_op jit(solution)/shard_map/while/body/eval_jaxpr/ppermute | solution.py:12
  111.9 6.8 %collective-permute-start.3 = (f32[128,128]{1,0:T(8,128)S(1)}, f32[128,128]{1,0:T(8,128)S(1)}, u32[]{:S(2)}, u32[]{:S(2)}) collective-permute-start(f32[128,128]{1,0:T(8,128)S(1)} %convolution_add_fusion.6), channel_id=1, source_target_pairs={{0,1},{1,2},{2,3},{3,4},{4,5},{5,6},{6,7},{7,8},{8,9},{9,10},{10,1... | collective-permute-start | bytes 196616 | tf_op jit(solution)/shard_map/while/body/eval_jaxpr/ppermute | solution.py:12
  118.7 6.0 %collective-permute-start = (bf16[128,128]{1,0:T(8,128)(2,1)S(1)}, bf16[128,128]{1,0:T(8,128)(2,1)S(1)}, u32[]{:S(2)}, u32[]{:S(2)}) collective-permute-start(bf16[128,128]{1,0:T(8,128)(2,1)S(1)} %copy.67), channel_id=1, source_target_pairs={{0,1},{1,2},{2,3},{3,4},{4,5},{5,6},{6,7},{7,8},{8,9},{9,10},{10,1... | collective-permute-start | bytes 98312 | tf_op jit(solution)/shard_map/while/body/eval_jaxpr/ppermute | solution.py:12
  118.7 6.4 %collective-permute-start.1 = (bf16[128,128]{1,0:T(8,128)(2,1)S(1)}, bf16[128,128]{1,0:T(8,128)(2,1)S(1)}, u32[]{:S(2)}, u32[]{:S(2)}) collective-permute-start(bf16[128,128]{1,0:T(8,128)(2,1)S(1)} %copy.68), channel_id=1, source_target_pairs={{0,1},{1,2},{2,3},{3,4},{4,5},{5,6},{6,7},{7,8},{8,9},{9,10},{10,1... | collective-permute-start | bytes 98312 | tf_op jit(solution)/shard_map/while/body/eval_jaxpr/ppermute | solution.py:12
  121.1 6.4 %collective-permute-start.2 = (f32[128,128]{1,0:T(8,128)S(1)}, f32[128,128]{1,0:T(8,128)S(1)}, u32[]{:S(2)}, u32[]{:S(2)}) collective-permute-start(f32[128,128]{1,0:T(8,128)S(1)} %fusion.122), channel_id=1, source_target_pairs={{0,1},{1,2},{2,3},{3,4},{4,5},{5,6},{6,7},{7,8},{8,9},{9,10},{10,1... | collective-permute-start | bytes 196616 | tf_op jit(solution)/shard_map/while/body/eval_jaxpr/ppermute | solution.py:12
  121.4 6.8 %collective-permute-start.3 = (f32[128,128]{1,0:T(8,128)S(1)}, f32[128,128]{1,0:T(8,128)S(1)}, u32[]{:S(2)}, u32[]{:S(2)}) collective-permute-start(f32[128,128]{1,0:T(8,128)S(1)} %convolution_add_fusion.6), channel_id=1, source_target_pairs={{0,1},{1,2},{2,3},{3,4},{4,5},{5,6},{6,7},{7,8},{8,9},{9,10},{10,1... | collective-permute-start | bytes 196616 | tf_op jit(solution)/shard_map/while/body/eval_jaxpr/ppermute | solution.py:12
  128.2 6.0 %collective-permute-start = (bf16[128,128]{1,0:T(8,128)(2,1)S(1)}, bf16[128,128]{1,0:T(8,128)(2,1)S(1)}, u32[]{:S(2)}, u32[]{:S(2)}) collective-permute-start(bf16[128,128]{1,0:T(8,128)(2,1)S(1)} %copy.67), channel_id=1, source_target_pairs={{0,1},{1,2},{2,3},{3,4},{4,5},{5,6},{6,7},{7,8},{8,9},{9,10},{10,1... | collective-permute-start | bytes 98312 | tf_op jit(solution)/shard_map/while/body/eval_jaxpr/ppermute | solution.py:12
  128.3 6.4 %collective-permute-start.1 = (bf16[128,128]{1,0:T(8,128)(2,1)S(1)}, bf16[128,128]{1,0:T(8,128)(2,1)S(1)}, u32[]{:S(2)}, u32[]{:S(2)}) collective-permute-start(bf16[128,128]{1,0:T(8,128)(2,1)S(1)} %copy.68), channel_id=1, source_target_pairs={{0,1},{1,2},{2,3},{3,4},{4,5},{5,6},{6,7},{7,8},{8,9},{9,10},{10,1... | collective-permute-start | bytes 98312 | tf_op jit(solution)/shard_map/while/body/eval_jaxpr/ppermute | solution.py:12
  130.6 6.4 %collective-permute-start.2 = (f32[128,128]{1,0:T(8,128)S(1)}, f32[128,128]{1,0:T(8,128)S(1)}, u32[]{:S(2)}, u32[]{:S(2)}) collective-permute-start(f32[128,128]{1,0:T(8,128)S(1)} %fusion.122), channel_id=1, source_target_pairs={{0,1},{1,2},{2,3},{3,4},{4,5},{5,6},{6,7},{7,8},{8,9},{9,10},{10,1... | collective-permute-start | bytes 196616 | tf_op jit(solution)/shard_map/while/body/eval_jaxpr/ppermute | solution.py:12
  130.9 6.8 %collective-permute-start.3 = (f32[128,128]{1,0:T(8,128)S(1)}, f32[128,128]{1,0:T(8,128)S(1)}, u32[]{:S(2)}, u32[]{:S(2)}) collective-permute-start(f32[128,128]{1,0:T(8,128)S(1)} %convolution_add_fusion.6), channel_id=1, source_target_pairs={{0,1},{1,2},{2,3},{3,4},{4,5},{5,6},{6,7},{7,8},{8,9},{9,10},{10,1... | collective-permute-start | bytes 196616 | tf_op jit(solution)/shard_map/while/body/eval_jaxpr/ppermute | solution.py:12
  137.8 6.0 %collective-permute-start = (bf16[128,128]{1,0:T(8,128)(2,1)S(1)}, bf16[128,128]{1,0:T(8,128)(2,1)S(1)}, u32[]{:S(2)}, u32[]{:S(2)}) collective-permute-start(bf16[128,128]{1,0:T(8,128)(2,1)S(1)} %copy.67), channel_id=1, source_target_pairs={{0,1},{1,2},{2,3},{3,4},{4,5},{5,6},{6,7},{7,8},{8,9},{9,10},{10,1... | collective-permute-start | bytes 98312 | tf_op jit(solution)/shard_map/while/body/eval_jaxpr/ppermute | solution.py:12
  137.8 6.4 %collective-permute-start.1 = (bf16[128,128]{1,0:T(8,128)(2,1)S(1)}, bf16[128,128]{1,0:T(8,128)(2,1)S(1)}, u32[]{:S(2)}, u32[]{:S(2)}) collective-permute-start(bf16[128,128]{1,0:T(8,128)(2,1)S(1)} %copy.68), channel_id=1, source_target_pairs={{0,1},{1,2},{2,3},{3,4},{4,5},{5,6},{6,7},{7,8},{8,9},{9,10},{10,1... | collective-permute-start | bytes 98312 | tf_op jit(solution)/shard_map/while/body/eval_jaxpr/ppermute | solution.py:12
  140.2 6.4 %collective-permute-start.2 = (f32[128,128]{1,0:T(8,128)S(1)}, f32[128,128]{1,0:T(8,128)S(1)}, u32[]{:S(2)}, u32[]{:S(2)}) collective-permute-start(f32[128,128]{1,0:T(8,128)S(1)} %fusion.122), channel_id=1, source_target_pairs={{0,1},{1,2},{2,3},{3,4},{4,5},{5,6},{6,7},{7,8},{8,9},{9,10},{10,1... | collective-permute-start | bytes 196616 | tf_op jit(solution)/shard_map/while/body/eval_jaxpr/ppermute | solution.py:12
  140.5 6.8 %collective-permute-start.3 = (f32[128,128]{1,0:T(8,128)S(1)}, f32[128,128]{1,0:T(8,128)S(1)}, u32[]{:S(2)}, u32[]{:S(2)}) collective-permute-start(f32[128,128]{1,0:T(8,128)S(1)} %convolution_add_fusion.6), channel_id=1, source_target_pairs={{0,1},{1,2},{2,3},{3,4},{4,5},{5,6},{6,7},{7,8},{8,9},{9,10},{10,1... | collective-permute-start | bytes 196616 | tf_op jit(solution)/shard_map/while/body/eval_jaxpr/ppermute | solution.py:12
  147.3 6.0 %collective-permute-start = (bf16[128,128]{1,0:T(8,128)(2,1)S(1)}, bf16[128,128]{1,0:T(8,128)(2,1)S(1)}, u32[]{:S(2)}, u32[]{:S(2)}) collective-permute-start(bf16[128,128]{1,0:T(8,128)(2,1)S(1)} %copy.67), channel_id=1, source_target_pairs={{0,1},{1,2},{2,3},{3,4},{4,5},{5,6},{6,7},{7,8},{8,9},{9,10},{10,1... | collective-permute-start | bytes 98312 | tf_op jit(solution)/shard_map/while/body/eval_jaxpr/ppermute | solution.py:12
  147.3 6.4 %collective-permute-start.1 = (bf16[128,128]{1,0:T(8,128)(2,1)S(1)}, bf16[128,128]{1,0:T(8,128)(2,1)S(1)}, u32[]{:S(2)}, u32[]{:S(2)}) collective-permute-start(bf16[128,128]{1,0:T(8,128)(2,1)S(1)} %copy.68), channel_id=1, source_target_pairs={{0,1},{1,2},{2,3},{3,4},{4,5},{5,6},{6,7},{7,8},{8,9},{9,10},{10,1... | collective-permute-start | bytes 98312 | tf_op jit(solution)/shard_map/while/body/eval_jaxpr/ppermute | solution.py:12
  149.7 6.4 %collective-permute-start.2 = (f32[128,128]{1,0:T(8,128)S(1)}, f32[128,128]{1,0:T(8,128)S(1)}, u32[]{:S(2)}, u32[]{:S(2)}) collective-permute-start(f32[128,128]{1,0:T(8,128)S(1)} %fusion.122), channel_id=1, source_target_pairs={{0,1},{1,2},{2,3},{3,4},{4,5},{5,6},{6,7},{7,8},{8,9},{9,10},{10,1... | collective-permute-start | bytes 196616 | tf_op jit(solution)/shard_map/while/body/eval_jaxpr/ppermute | solution.py:12
  150.0 6.8 %collective-permute-start.3 = (f32[128,128]{1,0:T(8,128)S(1)}, f32[128,128]{1,0:T(8,128)S(1)}, u32[]{:S(2)}, u32[]{:S(2)}) collective-permute-start(f32[128,128]{1,0:T(8,128)S(1)} %convolution_add_fusion.6), channel_id=1, source_target_pairs={{0,1},{1,2},{2,3},{3,4},{4,5},{5,6},{6,7},{7,8},{8,9},{9,10},{10,1... | collective-permute-start | bytes 196616 | tf_op jit(solution)/shard_map/while/body/eval_jaxpr/ppermute | solution.py:12
  156.8 6.0 %collective-permute-start = (bf16[128,128]{1,0:T(8,128)(2,1)S(1)}, bf16[128,128]{1,0:T(8,128)(2,1)S(1)}, u32[]{:S(2)}, u32[]{:S(2)}) collective-permute-start(bf16[128,128]{1,0:T(8,128)(2,1)S(1)} %copy.67), channel_id=1, source_target_pairs={{0,1},{1,2},{2,3},{3,4},{4,5},{5,6},{6,7},{7,8},{8,9},{9,10},{10,1... | collective-permute-start | bytes 98312 | tf_op jit(solution)/shard_map/while/body/eval_jaxpr/ppermute | solution.py:12
  156.9 6.4 %collective-permute-start.1 = (bf16[128,128]{1,0:T(8,128)(2,1)S(1)}, bf16[128,128]{1,0:T(8,128)(2,1)S(1)}, u32[]{:S(2)}, u32[]{:S(2)}) collective-permute-start(bf16[128,128]{1,0:T(8,128)(2,1)S(1)} %copy.68), channel_id=1, source_target_pairs={{0,1},{1,2},{2,3},{3,4},{4,5},{5,6},{6,7},{7,8},{8,9},{9,10},{10,1... | collective-permute-start | bytes 98312 | tf_op jit(solution)/shard_map/while/body/eval_jaxpr/ppermute | solution.py:12
  159.2 6.4 %collective-permute-start.2 = (f32[128,128]{1,0:T(8,128)S(1)}, f32[128,128]{1,0:T(8,128)S(1)}, u32[]{:S(2)}, u32[]{:S(2)}) collective-permute-start(f32[128,128]{1,0:T(8,128)S(1)} %fusion.122), channel_id=1, source_target_pairs={{0,1},{1,2},{2,3},{3,4},{4,5},{5,6},{6,7},{7,8},{8,9},{9,10},{10,1... | collective-permute-start | bytes 196616 | tf_op jit(solution)/shard_map/while/body/eval_jaxpr/ppermute | solution.py:12
  159.5 6.8 %collective-permute-start.3 = (f32[128,128]{1,0:T(8,128)S(1)}, f32[128,128]{1,0:T(8,128)S(1)}, u32[]{:S(2)}, u32[]{:S(2)}) collective-permute-start(f32[128,128]{1,0:T(8,128)S(1)} %convolution_add_fusion.6), channel_id=1, source_target_pairs={{0,1},{1,2},{2,3},{3,4},{4,5},{5,6},{6,7},{7,8},{8,9},{9,10},{10,1... | collective-permute-start | bytes 196616 | tf_op jit(solution)/shard_map/while/body/eval_jaxpr/ppermute | solution.py:12
  166.4 6.0 %collective-permute-start = (bf16[128,128]{1,0:T(8,128)(2,1)S(1)}, bf16[128,128]{1,0:T(8,128)(2,1)S(1)}, u32[]{:S(2)}, u32[]{:S(2)}) collective-permute-start(bf16[128,128]{1,0:T(8,128)(2,1)S(1)} %copy.67), channel_id=1, source_target_pairs={{0,1},{1,2},{2,3},{3,4},{4,5},{5,6},{6,7},{7,8},{8,9},{9,10},{10,1... | collective-permute-start | bytes 98312 | tf_op jit(solution)/shard_map/while/body/eval_jaxpr/ppermute | solution.py:12
  166.4 6.4 %collective-permute-start.1 = (bf16[128,128]{1,0:T(8,128)(2,1)S(1)}, bf16[128,128]{1,0:T(8,128)(2,1)S(1)}, u32[]{:S(2)}, u32[]{:S(2)}) collective-permute-start(bf16[128,128]{1,0:T(8,128)(2,1)S(1)} %copy.68), channel_id=1, source_target_pairs={{0,1},{1,2},{2,3},{3,4},{4,5},{5,6},{6,7},{7,8},{8,9},{9,10},{10,1... | collective-permute-start | bytes 98312 | tf_op jit(solution)/shard_map/while/body/eval_jaxpr/ppermute | solution.py:12
  168.8 6.4 %collective-permute-start.2 = (f32[128,128]{1,0:T(8,128)S(1)}, f32[128,128]{1,0:T(8,128)S(1)}, u32[]{:S(2)}, u32[]{:S(2)}) collective-permute-start(f32[128,128]{1,0:T(8,128)S(1)} %fusion.122), channel_id=1, source_target_pairs={{0,1},{1,2},{2,3},{3,4},{4,5},{5,6},{6,7},{7,8},{8,9},{9,10},{10,1... | collective-permute-start | bytes 196616 | tf_op jit(solution)/shard_map/while/body/eval_jaxpr/ppermute | solution.py:12
  169.1 6.8 %collective-permute-start.3 = (f32[128,128]{1,0:T(8,128)S(1)}, f32[128,128]{1,0:T(8,128)S(1)}, u32[]{:S(2)}, u32[]{:S(2)}) collective-permute-start(f32[128,128]{1,0:T(8,128)S(1)} %convolution_add_fusion.6), channel_id=1, source_target_pairs={{0,1},{1,2},{2,3},{3,4},{4,5},{5,6},{6,7},{7,8},{8,9},{9,10},{10,1... | collective-permute-start | bytes 196616 | tf_op jit(solution)/shard_map/while/body/eval_jaxpr/ppermute | solution.py:12
  175.9 6.0 %collective-permute-start = (bf16[128,128]{1,0:T(8,128)(2,1)S(1)}, bf16[128,128]{1,0:T(8,128)(2,1)S(1)}, u32[]{:S(2)}, u32[]{:S(2)}) collective-permute-start(bf16[128,128]{1,0:T(8,128)(2,1)S(1)} %copy.67), channel_id=1, source_target_pairs={{0,1},{1,2},{2,3},{3,4},{4,5},{5,6},{6,7},{7,8},{8,9},{9,10},{10,1... | collective-permute-start | bytes 98312 | tf_op jit(solution)/shard_map/while/body/eval_jaxpr/ppermute | solution.py:12
  175.9 6.4 %collective-permute-start.1 = (bf16[128,128]{1,0:T(8,128)(2,1)S(1)}, bf16[128,128]{1,0:T(8,128)(2,1)S(1)}, u32[]{:S(2)}, u32[]{:S(2)}) collective-permute-start(bf16[128,128]{1,0:T(8,128)(2,1)S(1)} %copy.68), channel_id=1, source_target_pairs={{0,1},{1,2},{2,3},{3,4},{4,5},{5,6},{6,7},{7,8},{8,9},{9,10},{10,1... | collective-permute-start | bytes 98312 | tf_op jit(solution)/shard_map/while/body/eval_jaxpr/ppermute | solution.py:12
  178.3 6.4 %collective-permute-start.2 = (f32[128,128]{1,0:T(8,128)S(1)}, f32[128,128]{1,0:T(8,128)S(1)}, u32[]{:S(2)}, u32[]{:S(2)}) collective-permute-start(f32[128,128]{1,0:T(8,128)S(1)} %fusion.122), channel_id=1, source_target_pairs={{0,1},{1,2},{2,3},{3,4},{4,5},{5,6},{6,7},{7,8},{8,9},{9,10},{10,1... | collective-permute-start | bytes 196616 | tf_op jit(solution)/shard_map/while/body/eval_jaxpr/ppermute | solution.py:12
  178.6 6.8 %collective-permute-start.3 = (f32[128,128]{1,0:T(8,128)S(1)}, f32[128,128]{1,0:T(8,128)S(1)}, u32[]{:S(2)}, u32[]{:S(2)}) collective-permute-start(f32[128,128]{1,0:T(8,128)S(1)} %convolution_add_fusion.6), channel_id=1, source_target_pairs={{0,1},{1,2},{2,3},{3,4},{4,5},{5,6},{6,7},{7,8},{8,9},{9,10},{10,1... | collective-permute-start | bytes 196616 | tf_op jit(solution)/shard_map/while/body/eval_jaxpr/ppermute | solution.py:12
  185.4 6.0 %collective-permute-start = (bf16[128,128]{1,0:T(8,128)(2,1)S(1)}, bf16[128,128]{1,0:T(8,128)(2,1)S(1)}, u32[]{:S(2)}, u32[]{:S(2)}) collective-permute-start(bf16[128,128]{1,0:T(8,128)(2,1)S(1)} %copy.67), channel_id=1, source_target_pairs={{0,1},{1,2},{2,3},{3,4},{4,5},{5,6},{6,7},{7,8},{8,9},{9,10},{10,1... | collective-permute-start | bytes 98312 | tf_op jit(solution)/shard_map/while/body/eval_jaxpr/ppermute | solution.py:12
  185.5 6.4 %collective-permute-start.1 = (bf16[128,128]{1,0:T(8,128)(2,1)S(1)}, bf16[128,128]{1,0:T(8,128)(2,1)S(1)}, u32[]{:S(2)}, u32[]{:S(2)}) collective-permute-start(bf16[128,128]{1,0:T(8,128)(2,1)S(1)} %copy.68), channel_id=1, source_target_pairs={{0,1},{1,2},{2,3},{3,4},{4,5},{5,6},{6,7},{7,8},{8,9},{9,10},{10,1... | collective-permute-start | bytes 98312 | tf_op jit(solution)/shard_map/while/body/eval_jaxpr/ppermute | solution.py:12
  187.8 6.4 %collective-permute-start.2 = (f32[128,128]{1,0:T(8,128)S(1)}, f32[128,128]{1,0:T(8,128)S(1)}, u32[]{:S(2)}, u32[]{:S(2)}) collective-permute-start(f32[128,128]{1,0:T(8,128)S(1)} %fusion.122), channel_id=1, source_target_pairs={{0,1},{1,2},{2,3},{3,4},{4,5},{5,6},{6,7},{7,8},{8,9},{9,10},{10,1... | collective-permute-start | bytes 196616 | tf_op jit(solution)/shard_map/while/body/eval_jaxpr/ppermute | solution.py:12
  188.1 6.8 %collective-permute-start.3 = (f32[128,128]{1,0:T(8,128)S(1)}, f32[128,128]{1,0:T(8,128)S(1)}, u32[]{:S(2)}, u32[]{:S(2)}) collective-permute-start(f32[128,128]{1,0:T(8,128)S(1)} %convolution_add_fusion.6), channel_id=1, source_target_pairs={{0,1},{1,2},{2,3},{3,4},{4,5},{5,6},{6,7},{7,8},{8,9},{9,10},{10,1... | collective-permute-start | bytes 196616 | tf_op jit(solution)/shard_map/while/body/eval_jaxpr/ppermute | solution.py:12
  195.0 6.0 %collective-permute-start = (bf16[128,128]{1,0:T(8,128)(2,1)S(1)}, bf16[128,128]{1,0:T(8,128)(2,1)S(1)}, u32[]{:S(2)}, u32[]{:S(2)}) collective-permute-start(bf16[128,128]{1,0:T(8,128)(2,1)S(1)} %copy.67), channel_id=1, source_target_pairs={{0,1},{1,2},{2,3},{3,4},{4,5},{5,6},{6,7},{7,8},{8,9},{9,10},{10,1... | collective-permute-start | bytes 98312 | tf_op jit(solution)/shard_map/while/body/eval_jaxpr/ppermute | solution.py:12
  195.0 6.4 %collective-permute-start.1 = (bf16[128,128]{1,0:T(8,128)(2,1)S(1)}, bf16[128,128]{1,0:T(8,128)(2,1)S(1)}, u32[]{:S(2)}, u32[]{:S(2)}) collective-permute-start(bf16[128,128]{1,0:T(8,128)(2,1)S(1)} %copy.68), channel_id=1, source_target_pairs={{0,1},{1,2},{2,3},{3,4},{4,5},{5,6},{6,7},{7,8},{8,9},{9,10},{10,1... | collective-permute-start | bytes 98312 | tf_op jit(solution)/shard_map/while/body/eval_jaxpr/ppermute | solution.py:12
  197.4 6.4 %collective-permute-start.2 = (f32[128,128]{1,0:T(8,128)S(1)}, f32[128,128]{1,0:T(8,128)S(1)}, u32[]{:S(2)}, u32[]{:S(2)}) collective-permute-start(f32[128,128]{1,0:T(8,128)S(1)} %fusion.122), channel_id=1, source_target_pairs={{0,1},{1,2},{2,3},{3,4},{4,5},{5,6},{6,7},{7,8},{8,9},{9,10},{10,1... | collective-permute-start | bytes 196616 | tf_op jit(solution)/shard_map/while/body/eval_jaxpr/ppermute | solution.py:12
  197.7 6.8 %collective-permute-start.3 = (f32[128,128]{1,0:T(8,128)S(1)}, f32[128,128]{1,0:T(8,128)S(1)}, u32[]{:S(2)}, u32[]{:S(2)}) collective-permute-start(f32[128,128]{1,0:T(8,128)S(1)} %convolution_add_fusion.6), channel_id=1, source_target_pairs={{0,1},{1,2},{2,3},{3,4},{4,5},{5,6},{6,7},{7,8},{8,9},{9,10},{10,1... | collective-permute-start | bytes 196616 | tf_op jit(solution)/shard_map/while/body/eval_jaxpr/ppermute | solution.py:12
  204.5 6.0 %collective-permute-start = (bf16[128,128]{1,0:T(8,128)(2,1)S(1)}, bf16[128,128]{1,0:T(8,128)(2,1)S(1)}, u32[]{:S(2)}, u32[]{:S(2)}) collective-permute-start(bf16[128,128]{1,0:T(8,128)(2,1)S(1)} %copy.67), channel_id=1, source_target_pairs={{0,1},{1,2},{2,3},{3,4},{4,5},{5,6},{6,7},{7,8},{8,9},{9,10},{10,1... | collective-permute-start | bytes 98312 | tf_op jit(solution)/shard_map/while/body/eval_jaxpr/ppermute | solution.py:12
  204.5 6.4 %collective-permute-start.1 = (bf16[128,128]{1,0:T(8,128)(2,1)S(1)}, bf16[128,128]{1,0:T(8,128)(2,1)S(1)}, u32[]{:S(2)}, u32[]{:S(2)}) collective-permute-start(bf16[128,128]{1,0:T(8,128)(2,1)S(1)} %copy.68), channel_id=1, source_target_pairs={{0,1},{1,2},{2,3},{3,4},{4,5},{5,6},{6,7},{7,8},{8,9},{9,10},{10,1... | collective-permute-start | bytes 98312 | tf_op jit(solution)/shard_map/while/body/eval_jaxpr/ppermute | solution.py:12
  206.9 6.4 %collective-permute-start.2 = (f32[128,128]{1,0:T(8,128)S(1)}, f32[128,128]{1,0:T(8,128)S(1)}, u32[]{:S(2)}, u32[]{:S(2)}) collective-permute-start(f32[128,128]{1,0:T(8,128)S(1)} %fusion.122), channel_id=1, source_target_pairs={{0,1},{1,2},{2,3},{3,4},{4,5},{5,6},{6,7},{7,8},{8,9},{9,10},{10,1... | collective-permute-start | bytes 196616 | tf_op jit(solution)/shard_map/while/body/eval_jaxpr/ppermute | solution.py:12
  207.2 6.8 %collective-permute-start.3 = (f32[128,128]{1,0:T(8,128)S(1)}, f32[128,128]{1,0:T(8,128)S(1)}, u32[]{:S(2)}, u32[]{:S(2)}) collective-permute-start(f32[128,128]{1,0:T(8,128)S(1)} %convolution_add_fusion.6), channel_id=1, source_target_pairs={{0,1},{1,2},{2,3},{3,4},{4,5},{5,6},{6,7},{7,8},{8,9},{9,10},{10,1... | collective-permute-start | bytes 196616 | tf_op jit(solution)/shard_map/while/body/eval_jaxpr/ppermute | solution.py:12
  214.5 6.4 %collective-permute-start.5 = (f32[128,128]{1,0:T(8,128)S(1)}, f32[128,128]{1,0:T(8,128)S(1)}, u32[]{:S(2)}, u32[]{:S(2)}) collective-permute-start(f32[128,128]{1,0:T(8,128)S(1)} %convolution_add_fusion.2), channel_id=1, source_target_pairs={{0,1},{1,2},{2,3},{3,4},{4,5},{5,6},{6,7},{7,8},{8,9},{9,10},{10,1... | collective-permute-start | bytes 196616 | tf_op jit(solution)/shard_map/ppermute | solution.py:12
  215.0 6.7 %collective-permute-start.4 = (f32[128,128]{1,0:T(8,128)S(1)}, f32[128,128]{1,0:T(8,128)S(1)}, u32[]{:S(2)}, u32[]{:S(2)}) collective-permute-start(f32[128,128]{1,0:T(8,128)S(1)} %fusion.45), channel_id=1, source_target_pairs={{0,1},{1,2},{2,3},{3,4},{4,5},{5,6},{6,7},{7,8},{8,9},{9,10},{10,1... | collective-permute-start | bytes 196616 | tf_op jit(solution)/shard_map/ppermute | solution.py:12
  (2 other events, 1.5 us)
where the time goes:
time: 223 us
  waiting for transfers between devices  103 us (46%)
  blocking collectives  43.4 us (19%)
  matrix products  31.7 us (14%)
  local copies, waits for them, and re-layouts  17 us (8%)
  loops' own time  13 us (6%)
  other arithmetic  5.81 us (3%)
  starting transfers between devices  5 us (2%)
  between operations  4.08 us (2%)
    ppermute x62, waiting for transfers between devices, passed_along(): return lax.ppermute(value, axis, pairs)  103 us
    all_gather x1, blocking collectives, shards(): key_piece = lax.all_gather(key_states, 'blk', axis=0, tiled=True)  24.6 us
    all_gather x1, blocking collectives, shards(): value_piece = lax.all_gather(value_states, 'blk', axis=0, tiled=True)  18.9 us
    another operation x1, loops' own time, shards(): carry_state = lax.fori_loop(0, cycle_size - 1, key_turn, carry_state)  11.7 us
    dynamic_slice x16, local copies, waits for them, and re-layouts, key_step(): key_pos = block_order[source] * tok_rows + offsets  9.38 us
    dot_general x32, matrix products, mask_for(): jnp.dot(tile_rows, one_hot.T, preferred_element_type=jnp.float32) > 0.5  6.53 us
    ppermute x62, starting transfers between devices, passed_along(): return lax.ppermute(value, axis, pairs)  5 us
    dot_general x16, matrix products, softmax_update(): jnp.dot(weights.astype(jnp.bfloat16), value_sub, preferred_element_type=j...  4.83 us
  transfers between devices with their start and end apart: 62, of which 62 were waited for; matrix products, arithmetic and copies ran while one was open for 14% of the time, Pallas kernels for 0%

commit v1 on v0

--- a/solution.py
+++ b/solution.py
@@ -80,8 +80,13 @@
         jnp.zeros((total_rows,), jnp.float32),
         jnp.zeros((total_rows, head_width), jnp.float32),
     )
-    key_piece = lax.all_gather(key_states, "blk", axis=0, tiled=True)
-    value_piece = lax.all_gather(value_states, "blk", axis=0, tiled=True)
+    key_piece, value_piece = jnp.split(
+        lax.all_gather(
+            jnp.concatenate([key_states, value_states], axis=1), "blk", axis=0, tiled=True
+        ),
+        [key_states.shape[1]],
+        axis=1,
+    )
     piece_rows = key_piece.shape[0]
 
     def sub_step(sub_num, inner_state):

time: 223 us -> 230 us (1.031)
  blocking collectives: 43.4 us -> 0 us
  waiting for transfers between devices: 103 us -> 136 us
  between operations: 4.08 us -> 17.4 us
    all_gather x2 -> x0, blocking collectives: 43.4 us -> none  [the longest x1 24.6 us: shards(): key_piece = lax.all_gather(key_states, 'blk', axis=0, tiled=True)]
    all_gather x0 -> x1, waiting for transfers between devices: none -> 35.6 us  [shards(): lax.all_gather(jnp.concatenate([key_states, value_states], axis=1), 'blk'...]
  transfers between devices with their start and end apart: 62 -> 63, of which waited for: 62 -> 63; matrix products, arithmetic and copies ran while one was open for 14% -> 15% of each run, Pallas kernels for 0% -> 0%
where the time goes in v1:
time: 230 us
  waiting for transfers between devices  136 us (59%)
  matrix products  31.7 us (14%)
  local copies, waits for them, and re-layouts  19.1 us (8%)
  between operations  17.4 us (8%)
  loops' own time  13 us (6%)
  other arithmetic  6.46 us (3%)
  starting transfers between devices  5.98 us (3%)
    ppermute x62, waiting for transfers between devices, passed_along(): return lax.ppermute(value, axis, pairs)  101 us
    all_gather x1, waiting for transfers between devices, shards(): lax.all_gather(jnp.concatenate([key_states, value_states], axis=1), 'blk'...  35.6 us
    another operation x1, loops' own time, shards(): carry_state = lax.fori_loop(0, cycle_size - 1, key_turn, carry_state)  11.7 us
    dynamic_slice x16, local copies, waits for them, and re-layouts, key_step(): key_pos = block_order[source] * tok_rows + offsets  9.4 us
    dot_general x32, matrix products, mask_for(): jnp.dot(tile_rows, one_hot.T, preferred_element_type=jnp.float32) > 0.5  6.53 us
    ppermute x62, starting transfers between devices, passed_along(): return lax.ppermute(value, axis, pairs)  5.94 us
    dot_general x16, matrix products, softmax_update(): jnp.dot(weights.astype(jnp.bfloat16), value_sub, preferred_element_type=j...  4.83 us
  transfers between devices with their start and end apart: 63, of which 63 were waited for; matrix products, arithmetic and copies ran while one was open for 15% of the time, Pallas kernels for 0%

profile of v1, /device:TPU:0, one launch (start us, length us, event | category | flops | bytes accessed | tf_op | source)
XLA Modules:
  0.0 229.9 jit_solution(13838574433919404490)
XLA Ops:
  7.2 0.8 copy.83
  8.0 0.6 pad_maximum_fusion
  8.7 0.6 copy-done.3
  9.3 0.6 fusion.54
  13.1 0.7 fusion.74
  14.2 0.7 dynamic-slice_convert_fusion
  15.0 0.9 copy-done.1
  15.9 35.6 %all-gather.2.cloned.1.call-done = bf16[2048,256]{1,0:T(8,128)(2,1)} async-done(((bf16[128,256]{1,0:T(8,128)(2,1)}), bf16[2048,256]{1,0:T(8,128)(2,1)}) %all-gather.2.cloned.1.call-update) | async-done | bytes 1048592 | tf_op jit(solution)/shard_map/all_gather | solution.py:84
  51.4 1.3 fusion.53
  52.7 17.7 %while.47 = (s32[]{:T(128)}, f32[512]{0:T(512)S(1)}, f32[512]{0:T(512)S(1)}, f32[512,128]{1,0:T(8,128)S(1)}, s32[]{:T(128)}, /*index=5*/s32[16]{0:T(128)S(1)}, b...) while((s32[]{:T(128)}, f32[512]{0:T(512)S(1)}, ...), condition=%wide.region_4.5_spmd.clone, body=%wide.region_0.4_spmd.clone.sunk | while | flops 34965508 | bytes 1841459 | solution.py:109
  70.6 143.6 %while.48 = (s32[]{:T(128)}, bf16[128,128]{1,0:T(8,128)(2,1)S(1)}, bf16[128,128]{1,0:T(8,128)(2,1)S(1)}, f32[128,128]{1,0:T(8,128)S(1)}, f32[128,128]{1,0:T(8,12...) while((s32[]{:T(128)}, bf16[128,128]{1,0:T(8,128)(2,1)S(1)}, ...), condition=%wide.region_7.8_spmd.clone.clone, body=%wide.region_6.7_spmd.clone.clone.sunk | while | flops 85202960 | bytes 3711538 | solution.py:160
  74.2 1.4 collective-permute-start.3
  75.8 1.0 collective-permute-done
  77.1 3.0 %collective-permute-done.2 = f32[128,128]{1,0:T(8,128)S(1)} collective-permute-done((f32[128,128]{1,0:T(8,128)S(1)}, f32[128,128]{1,0:T(8,128)S(1)}, u32[]{:S(2)}, u32[]{:S(2)}) %collective-permute-start.2) | collective-permute-done | bytes 65568 | tf_op jit(solution)/shard_map/while/body/eval_jaxpr/ppermute | solution.py:12
  80.1 0.7 collective-permute-done.3
  83.5 1.1 collective-permute-start.3
  84.7 2.1 collective-permute-done
  87.2 2.4 %collective-permute-done.2 = f32[128,128]{1,0:T(8,128)S(1)} collective-permute-done((f32[128,128]{1,0:T(8,128)S(1)}, f32[128,128]{1,0:T(8,128)S(1)}, u32[]{:S(2)}, u32[]{:S(2)}) %collective-permute-start.2) | collective-permute-done | bytes 65568 | tf_op jit(solution)/shard_map/while/body/eval_jaxpr/ppermute | solution.py:12
  89.6 0.7 collective-permute-done.3
  93.3 3.1 %collective-permute-done = bf16[128,128]{1,0:T(8,128)(2,1)S(1)} collective-permute-done((bf16[128,128]{1,0:T(8,128)(2,1)S(1)}, bf16[128,128]{1,0:T(8,128)(2,1)S(1)}, u32[]{:S(2)}, u32[]{:S(2)}) %collective-permute-start) | collective-permute-done | bytes 32800 | tf_op jit(solution)/shard_map/while/body/eval_jaxpr/ppermute | solution.py:12
  96.7 2.4 %collective-permute-done.2 = f32[128,128]{1,0:T(8,128)S(1)} collective-permute-done((f32[128,128]{1,0:T(8,128)S(1)}, f32[128,128]{1,0:T(8,128)S(1)}, u32[]{:S(2)}, u32[]{:S(2)}) %collective-permute-start.2) | collective-permute-done | bytes 65568 | tf_op jit(solution)/shard_map/while/body/eval_jaxpr/ppermute | solution.py:12
  99.1 0.7 collective-permute-done.3
  102.8 3.1 %collective-permute-done = bf16[128,128]{1,0:T(8,128)(2,1)S(1)} collective-permute-done((bf16[128,128]{1,0:T(8,128)(2,1)S(1)}, bf16[128,128]{1,0:T(8,128)(2,1)S(1)}, u32[]{:S(2)}, u32[]{:S(2)}) %collective-permute-start) | collective-permute-done | bytes 32800 | tf_op jit(solution)/shard_map/while/body/eval_jaxpr/ppermute | solution.py:12
  106.2 2.4 %collective-permute-done.2 = f32[128,128]{1,0:T(8,128)S(1)} collective-permute-done((f32[128,128]{1,0:T(8,128)S(1)}, f32[128,128]{1,0:T(8,128)S(1)}, u32[]{:S(2)}, u32[]{:S(2)}) %collective-permute-start.2) | collective-permute-done | bytes 65568 | tf_op jit(solution)/shard_map/while/body/eval_jaxpr/ppermute | solution.py:12
  108.7 0.7 collective-permute-done.3
  112.3 3.1 %collective-permute-done = bf16[128,128]{1,0:T(8,128)(2,1)S(1)} collective-permute-done((bf16[128,128]{1,0:T(8,128)(2,1)S(1)}, bf16[128,128]{1,0:T(8,128)(2,1)S(1)}, u32[]{:S(2)}, u32[]{:S(2)}) %collective-permute-start) | collective-permute-done | bytes 32800 | tf_op jit(solution)/shard_map/while/body/eval_jaxpr/ppermute | solution.py:12
  115.8 2.4 %collective-permute-done.2 = f32[128,128]{1,0:T(8,128)S(1)} collective-permute-done((f32[128,128]{1,0:T(8,128)S(1)}, f32[128,128]{1,0:T(8,128)S(1)}, u32[]{:S(2)}, u32[]{:S(2)}) %collective-permute-start.2) | collective-permute-done | bytes 65568 | tf_op jit(solution)/shard_map/while/body/eval_jaxpr/ppermute | solution.py:12
  118.2 0.7 collective-permute-done.3
  121.9 3.1 %collective-permute-done = bf16[128,128]{1,0:T(8,128)(2,1)S(1)} collective-permute-done((bf16[128,128]{1,0:T(8,128)(2,1)S(1)}, bf16[128,128]{1,0:T(8,128)(2,1)S(1)}, u32[]{:S(2)}, u32[]{:S(2)}) %collective-permute-start) | collective-permute-done | bytes 32800 | tf_op jit(solution)/shard_map/while/body/eval_jaxpr/ppermute | solution.py:12
  125.3 2.4 %collective-permute-done.2 = f32[128,128]{1,0:T(8,128)S(1)} collective-permute-done((f32[128,128]{1,0:T(8,128)S(1)}, f32[128,128]{1,0:T(8,128)S(1)}, u32[]{:S(2)}, u32[]{:S(2)}) %collective-permute-start.2) | collective-permute-done | bytes 65568 | tf_op jit(solution)/shard_map/while/body/eval_jaxpr/ppermute | solution.py:12
  127.7 0.7 collective-permute-done.3
  131.4 3.1 %collective-permute-done = bf16[128,128]{1,0:T(8,128)(2,1)S(1)} collective-permute-done((bf16[128,128]{1,0:T(8,128)(2,1)S(1)}, bf16[128,128]{1,0:T(8,128)(2,1)S(1)}, u32[]{:S(2)}, u32[]{:S(2)}) %collective-permute-start) | collective-permute-done | bytes 32800 | tf_op jit(solution)/shard_map/while/body/eval_jaxpr/ppermute | solution.py:12
  134.8 2.4 %collective-permute-done.2 = f32[128,128]{1,0:T(8,128)S(1)} collective-permute-done((f32[128,128]{1,0:T(8,128)S(1)}, f32[128,128]{1,0:T(8,128)S(1)}, u32[]{:S(2)}, u32[]{:S(2)}) %collective-permute-start.2) | collective-permute-done | bytes 65568 | tf_op jit(solution)/shard_map/while/body/eval_jaxpr/ppermute | solution.py:12
  137.3 0.7 collective-permute-done.3
  140.9 3.1 %collective-permute-done = bf16[128,128]{1,0:T(8,128)(2,1)S(1)} collective-permute-done((bf16[128,128]{1,0:T(8,128)(2,1)S(1)}, bf16[128,128]{1,0:T(8,128)(2,1)S(1)}, u32[]{:S(2)}, u32[]{:S(2)}) %collective-permute-start) | collective-permute-done | bytes 32800 | tf_op jit(solution)/shard_map/while/body/eval_jaxpr/ppermute | solution.py:12
  144.3 2.4 %collective-permute-done.2 = f32[128,128]{1,0:T(8,128)S(1)} collective-permute-done((f32[128,128]{1,0:T(8,128)S(1)}, f32[128,128]{1,0:T(8,128)S(1)}, u32[]{:S(2)}, u32[]{:S(2)}) %collective-permute-start.2) | collective-permute-done | bytes 65568 | tf_op jit(solution)/shard_map/while/body/eval_jaxpr/ppermute | solution.py:12
  146.8 0.7 collective-permute-done.3
  150.5 3.1 %collective-permute-done = bf16[128,128]{1,0:T(8,128)(2,1)S(1)} collective-permute-done((bf16[128,128]{1,0:T(8,128)(2,1)S(1)}, bf16[128,128]{1,0:T(8,128)(2,1)S(1)}, u32[]{:S(2)}, u32[]{:S(2)}) %collective-permute-start) | collective-permute-done | bytes 32800 | tf_op jit(solution)/shard_map/while/body/eval_jaxpr/ppermute | solution.py:12
  153.9 2.4 %collective-permute-done.2 = f32[128,128]{1,0:T(8,128)S(1)} collective-permute-done((f32[128,128]{1,0:T(8,128)S(1)}, f32[128,128]{1,0:T(8,128)S(1)}, u32[]{:S(2)}, u32[]{:S(2)}) %collective-permute-start.2) | collective-permute-done | bytes 65568 | tf_op jit(solution)/shard_map/while/body/eval_jaxpr/ppermute | solution.py:12
  156.3 0.7 collective-permute-done.3
  160.0 3.1 %collective-permute-done = bf16[128,128]{1,0:T(8,128)(2,1)S(1)} collective-permute-done((bf16[128,128]{1,0:T(8,128)(2,1)S(1)}, bf16[128,128]{1,0:T(8,128)(2,1)S(1)}, u32[]{:S(2)}, u32[]{:S(2)}) %collective-permute-start) | collective-permute-done | bytes 32800 | tf_op jit(solution)/shard_map/while/body/eval_jaxpr/ppermute | solution.py:12
  163.4 2.4 %collective-permute-done.2 = f32[128,128]{1,0:T(8,128)S(1)} collective-permute-done((f32[128,128]{1,0:T(8,128)S(1)}, f32[128,128]{1,0:T(8,128)S(1)}, u32[]{:S(2)}, u32[]{:S(2)}) %collective-permute-start.2) | collective-permute-done | bytes 65568 | tf_op jit(solution)/shard_map/while/body/eval_jaxpr/ppermute | solution.py:12
  165.8 0.7 collective-permute-done.3
  169.5 3.1 %collective-permute-done = bf16[128,128]{1,0:T(8,128)(2,1)S(1)} collective-permute-done((bf16[128,128]{1,0:T(8,128)(2,1)S(1)}, bf16[128,128]{1,0:T(8,128)(2,1)S(1)}, u32[]{:S(2)}, u32[]{:S(2)}) %collective-permute-start) | collective-permute-done | bytes 32800 | tf_op jit(solution)/shard_map/while/body/eval_jaxpr/ppermute | solution.py:12
  172.9 2.4 %collective-permute-done.2 = f32[128,128]{1,0:T(8,128)S(1)} collective-permute-done((f32[128,128]{1,0:T(8,128)S(1)}, f32[128,128]{1,0:T(8,128)S(1)}, u32[]{:S(2)}, u32[]{:S(2)}) %collective-permute-start.2) | collective-permute-done | bytes 65568 | tf_op jit(solution)/shard_map/while/body/eval_jaxpr/ppermute | solution.py:12
  175.4 0.7 collective-permute-done.3
  179.1 3.1 %collective-permute-done = bf16[128,128]{1,0:T(8,128)(2,1)S(1)} collective-permute-done((bf16[128,128]{1,0:T(8,128)(2,1)S(1)}, bf16[128,128]{1,0:T(8,128)(2,1)S(1)}, u32[]{:S(2)}, u32[]{:S(2)}) %collective-permute-start) | collective-permute-done | bytes 32800 | tf_op jit(solution)/shard_map/while/body/eval_jaxpr/ppermute | solution.py:12
  182.5 2.4 %collective-permute-done.2 = f32[128,128]{1,0:T(8,128)S(1)} collective-permute-done((f32[128,128]{1,0:T(8,128)S(1)}, f32[128,128]{1,0:T(8,128)S(1)}, u32[]{:S(2)}, u32[]{:S(2)}) %collective-permute-start.2) | collective-permute-done | bytes 65568 | tf_op jit(solution)/shard_map/while/body/eval_jaxpr/ppermute | solution.py:12
  184.9 0.7 collective-permute-done.3
  188.6 3.1 %collective-permute-done = bf16[128,128]{1,0:T(8,128)(2,1)S(1)} collective-permute-done((bf16[128,128]{1,0:T(8,128)(2,1)S(1)}, bf16[128,128]{1,0:T(8,128)(2,1)S(1)}, u32[]{:S(2)}, u32[]{:S(2)}) %collective-permute-start) | collective-permute-done | bytes 32800 | tf_op jit(solution)/shard_map/while/body/eval_jaxpr/ppermute | solution.py:12
  192.0 2.4 %collective-permute-done.2 = f32[128,128]{1,0:T(8,128)S(1)} collective-permute-done((f32[128,128]{1,0:T(8,128)S(1)}, f32[128,128]{1,0:T(8,128)S(1)}, u32[]{:S(2)}, u32[]{:S(2)}) %collective-permute-start.2) | collective-permute-done | bytes 65568 | tf_op jit(solution)/shard_map/while/body/eval_jaxpr/ppermute | solution.py:12
  194.4 0.7 collective-permute-done.3
  198.1 3.1 %collective-permute-done = bf16[128,128]{1,0:T(8,128)(2,1)S(1)} collective-permute-done((bf16[128,128]{1,0:T(8,128)(2,1)S(1)}, bf16[128,128]{1,0:T(8,128)(2,1)S(1)}, u32[]{:S(2)}, u32[]{:S(2)}) %collective-permute-start) | collective-permute-done | bytes 32800 | tf_op jit(solution)/shard_map/while/body/eval_jaxpr/ppermute | solution.py:12
  201.5 2.4 %collective-permute-done.2 = f32[128,128]{1,0:T(8,128)S(1)} collective-permute-done((f32[128,128]{1,0:T(8,128)S(1)}, f32[128,128]{1,0:T(8,128)S(1)}, u32[]{:S(2)}, u32[]{:S(2)}) %collective-permute-start.2) | collective-permute-done | bytes 65568 | tf_op jit(solution)/shard_map/while/body/eval_jaxpr/ppermute | solution.py:12
  204.0 0.7 collective-permute-done.3
  207.7 3.1 %collective-permute-done = bf16[128,128]{1,0:T(8,128)(2,1)S(1)} collective-permute-done((bf16[128,128]{1,0:T(8,128)(2,1)S(1)}, bf16[128,128]{1,0:T(8,128)(2,1)S(1)}, u32[]{:S(2)}, u32[]{:S(2)}) %collective-permute-start) | collective-permute-done | bytes 32800 | tf_op jit(solution)/shard_map/while/body/eval_jaxpr/ppermute | solution.py:12
  211.1 2.4 %collective-permute-done.2 = f32[128,128]{1,0:T(8,128)S(1)} collective-permute-done((f32[128,128]{1,0:T(8,128)S(1)}, f32[128,128]{1,0:T(8,128)S(1)}, u32[]{:S(2)}, u32[]{:S(2)}) %collective-permute-start.2) | collective-permute-done | bytes 65568 | tf_op jit(solution)/shard_map/while/body/eval_jaxpr/ppermute | solution.py:12
  213.5 0.7 collective-permute-done.3
  215.4 0.7 copy.41
  216.2 0.7 copy.40
  216.9 4.2 %collective-permute-done.5 = f32[128,128]{1,0:T(8,128)S(1)} collective-permute-done((f32[128,128]{1,0:T(8,128)S(1)}, f32[128,128]{1,0:T(8,128)S(1)}, u32[]{:S(2)}, u32[]{:S(2)}) %collective-permute-start.5) | collective-permute-done | bytes 65568 | tf_op jit(solution)/shard_map/ppermute | solution.py:12
  221.1 0.7 collective-permute-done.4
  221.8 0.6 copy.85
  222.5 0.6 copy.86
  (492 shorter events, 57.3 us)
Async XLA Ops:
  7.2 7.8 %copy-start = (bf16[128,512]{1,0:T(8,128)(2,1)S(1)}, bf16[128,512]{1,0:T(8,128)(2,1)}, u32[]{:S(2)}) copy-start(bf16[128,512]{1,0:T(8,128)(2,1)} %param.10) | copy-start | bytes 393220
  7.2 44.2 %all-gather.2.cloned.1.call-start = ((), (), s32[]{:S(2)}) async-start(), calls=%async_computation | async-start | bytes 1114112 | tf_op jit(solution)/shard_map/all_gather | solution.py:84
  70.7 6.1 %collective-permute-start = (bf16[128,128]{1,0:T(8,128)(2,1)S(1)}, bf16[128,128]{1,0:T(8,128)(2,1)S(1)}, u32[]{:S(2)}, u32[]{:S(2)}) collective-permute-start(bf16[128,128]{1,0:T(8,128)(2,1)S(1)} %copy.67), channel_id=1, source_target_pairs={{0,1},{1,2},{2,3},{3,4},{4,5},{5,6},{6,7},{7,8},{8,9},{9,10},{10,1... | collective-permute-start | bytes 98312 | tf_op jit(solution)/shard_map/while/body/eval_jaxpr/ppermute | solution.py:12
  71.0 6.1 %collective-permute-start.1 = (bf16[128,128]{1,0:T(8,128)(2,1)S(1)}, bf16[128,128]{1,0:T(8,128)(2,1)S(1)}, u32[]{:S(2)}, u32[]{:S(2)}) collective-permute-start(bf16[128,128]{1,0:T(8,128)(2,1)S(1)} %copy.68), channel_id=1, source_target_pairs={{0,1},{1,2},{2,3},{3,4},{4,5},{5,6},{6,7},{7,8},{8,9},{9,10},{10,1... | collective-permute-start | bytes 98312 | tf_op jit(solution)/shard_map/while/body/eval_jaxpr/ppermute | solution.py:12
  73.6 6.4 %collective-permute-start.2 = (f32[128,128]{1,0:T(8,128)S(1)}, f32[128,128]{1,0:T(8,128)S(1)}, u32[]{:S(2)}, u32[]{:S(2)}) collective-permute-start(f32[128,128]{1,0:T(8,128)S(1)} %fusion.123), channel_id=1, source_target_pairs={{0,1},{1,2},{2,3},{3,4},{4,5},{5,6},{6,7},{7,8},{8,9},{9,10},{10,1... | collective-permute-start | bytes 196616 | tf_op jit(solution)/shard_map/while/body/eval_jaxpr/ppermute | solution.py:12
  74.2 6.6 %collective-permute-start.3 = (f32[128,128]{1,0:T(8,128)S(1)}, f32[128,128]{1,0:T(8,128)S(1)}, u32[]{:S(2)}, u32[]{:S(2)}) collective-permute-start(f32[128,128]{1,0:T(8,128)S(1)} %convolution_add_fusion.6), channel_id=1, source_target_pairs={{0,1},{1,2},{2,3},{3,4},{4,5},{5,6},{6,7},{7,8},{8,9},{9,10},{10,1... | collective-permute-start | bytes 196616 | tf_op jit(solution)/shard_map/while/body/eval_jaxpr/ppermute | solution.py:12
  80.8 6.0 %collective-permute-start = (bf16[128,128]{1,0:T(8,128)(2,1)S(1)}, bf16[128,128]{1,0:T(8,128)(2,1)S(1)}, u32[]{:S(2)}, u32[]{:S(2)}) collective-permute-start(bf16[128,128]{1,0:T(8,128)(2,1)S(1)} %copy.67), channel_id=1, source_target_pairs={{0,1},{1,2},{2,3},{3,4},{4,5},{5,6},{6,7},{7,8},{8,9},{9,10},{10,1... | collective-permute-start | bytes 98312 | tf_op jit(solution)/shard_map/while/body/eval_jaxpr/ppermute | solution.py:12
  80.8 6.4 %collective-permute-start.1 = (bf16[128,128]{1,0:T(8,128)(2,1)S(1)}, bf16[128,128]{1,0:T(8,128)(2,1)S(1)}, u32[]{:S(2)}, u32[]{:S(2)}) collective-permute-start(bf16[128,128]{1,0:T(8,128)(2,1)S(1)} %copy.68), channel_id=1, source_target_pairs={{0,1},{1,2},{2,3},{3,4},{4,5},{5,6},{6,7},{7,8},{8,9},{9,10},{10,1... | collective-permute-start | bytes 98312 | tf_op jit(solution)/shard_map/while/body/eval_jaxpr/ppermute | solution.py:12
  83.2 6.4 %collective-permute-start.2 = (f32[128,128]{1,0:T(8,128)S(1)}, f32[128,128]{1,0:T(8,128)S(1)}, u32[]{:S(2)}, u32[]{:S(2)}) collective-permute-start(f32[128,128]{1,0:T(8,128)S(1)} %fusion.123), channel_id=1, source_target_pairs={{0,1},{1,2},{2,3},{3,4},{4,5},{5,6},{6,7},{7,8},{8,9},{9,10},{10,1... | collective-permute-start | bytes 196616 | tf_op jit(solution)/shard_map/while/body/eval_jaxpr/ppermute | solution.py:12
  83.5 6.8 %collective-permute-start.3 = (f32[128,128]{1,0:T(8,128)S(1)}, f32[128,128]{1,0:T(8,128)S(1)}, u32[]{:S(2)}, u32[]{:S(2)}) collective-permute-start(f32[128,128]{1,0:T(8,128)S(1)} %convolution_add_fusion.6), channel_id=1, source_target_pairs={{0,1},{1,2},{2,3},{3,4},{4,5},{5,6},{6,7},{7,8},{8,9},{9,10},{10,1... | collective-permute-start | bytes 196616 | tf_op jit(solution)/shard_map/while/body/eval_jaxpr/ppermute | solution.py:12
  90.3 6.0 %collective-permute-start = (bf16[128,128]{1,0:T(8,128)(2,1)S(1)}, bf16[128,128]{1,0:T(8,128)(2,1)S(1)}, u32[]{:S(2)}, u32[]{:S(2)}) collective-permute-start(bf16[128,128]{1,0:T(8,128)(2,1)S(1)} %copy.67), channel_id=1, source_target_pairs={{0,1},{1,2},{2,3},{3,4},{4,5},{5,6},{6,7},{7,8},{8,9},{9,10},{10,1... | collective-permute-start | bytes 98312 | tf_op jit(solution)/shard_map/while/body/eval_jaxpr/ppermute | solution.py:12
  90.3 6.4 %collective-permute-start.1 = (bf16[128,128]{1,0:T(8,128)(2,1)S(1)}, bf16[128,128]{1,0:T(8,128)(2,1)S(1)}, u32[]{:S(2)}, u32[]{:S(2)}) collective-permute-start(bf16[128,128]{1,0:T(8,128)(2,1)S(1)} %copy.68), channel_id=1, source_target_pairs={{0,1},{1,2},{2,3},{3,4},{4,5},{5,6},{6,7},{7,8},{8,9},{9,10},{10,1... | collective-permute-start | bytes 98312 | tf_op jit(solution)/shard_map/while/body/eval_jaxpr/ppermute | solution.py:12
  92.7 6.4 %collective-permute-start.2 = (f32[128,128]{1,0:T(8,128)S(1)}, f32[128,128]{1,0:T(8,128)S(1)}, u32[]{:S(2)}, u32[]{:S(2)}) collective-permute-start(f32[128,128]{1,0:T(8,128)S(1)} %fusion.123), channel_id=1, source_target_pairs={{0,1},{1,2},{2,3},{3,4},{4,5},{5,6},{6,7},{7,8},{8,9},{9,10},{10,1... | collective-permute-start | bytes 196616 | tf_op jit(solution)/shard_map/while/body/eval_jaxpr/ppermute | solution.py:12
  93.0 6.8 %collective-permute-start.3 = (f32[128,128]{1,0:T(8,128)S(1)}, f32[128,128]{1,0:T(8,128)S(1)}, u32[]{:S(2)}, u32[]{:S(2)}) collective-permute-start(f32[128,128]{1,0:T(8,128)S(1)} %convolution_add_fusion.6), channel_id=1, source_target_pairs={{0,1},{1,2},{2,3},{3,4},{4,5},{5,6},{6,7},{7,8},{8,9},{9,10},{10,1... | collective-permute-start | bytes 196616 | tf_op jit(solution)/shard_map/while/body/eval_jaxpr/ppermute | solution.py:12
  99.8 6.0 %collective-permute-start = (bf16[128,128]{1,0:T(8,128)(2,1)S(1)}, bf16[128,128]{1,0:T(8,128)(2,1)S(1)}, u32[]{:S(2)}, u32[]{:S(2)}) collective-permute-start(bf16[128,128]{1,0:T(8,128)(2,1)S(1)} %copy.67), channel_id=1, source_target_pairs={{0,1},{1,2},{2,3},{3,4},{4,5},{5,6},{6,7},{7,8},{8,9},{9,10},{10,1... | collective-permute-start | bytes 98312 | tf_op jit(solution)/shard_map/while/body/eval_jaxpr/ppermute | solution.py:12
  99.8 6.4 %collective-permute-start.1 = (bf16[128,128]{1,0:T(8,128)(2,1)S(1)}, bf16[128,128]{1,0:T(8,128)(2,1)S(1)}, u32[]{:S(2)}, u32[]{:S(2)}) collective-permute-start(bf16[128,128]{1,0:T(8,128)(2,1)S(1)} %copy.68), channel_id=1, source_target_pairs={{0,1},{1,2},{2,3},{3,4},{4,5},{5,6},{6,7},{7,8},{8,9},{9,10},{10,1... | collective-permute-start | bytes 98312 | tf_op jit(solution)/shard_map/while/body/eval_jaxpr/ppermute | solution.py:12
  102.2 6.4 %collective-permute-start.2 = (f32[128,128]{1,0:T(8,128)S(1)}, f32[128,128]{1,0:T(8,128)S(1)}, u32[]{:S(2)}, u32[]{:S(2)}) collective-permute-start(f32[128,128]{1,0:T(8,128)S(1)} %fusion.123), channel_id=1, source_target_pairs={{0,1},{1,2},{2,3},{3,4},{4,5},{5,6},{6,7},{7,8},{8,9},{9,10},{10,1... | collective-permute-start | bytes 196616 | tf_op jit(solution)/shard_map/while/body/eval_jaxpr/ppermute | solution.py:12
  102.5 6.8 %collective-permute-start.3 = (f32[128,128]{1,0:T(8,128)S(1)}, f32[128,128]{1,0:T(8,128)S(1)}, u32[]{:S(2)}, u32[]{:S(2)}) collective-permute-start(f32[128,128]{1,0:T(8,128)S(1)} %convolution_add_fusion.6), channel_id=1, source_target_pairs={{0,1},{1,2},{2,3},{3,4},{4,5},{5,6},{6,7},{7,8},{8,9},{9,10},{10,1... | collective-permute-start | bytes 196616 | tf_op jit(solution)/shard_map/while/body/eval_jaxpr/ppermute | solution.py:12
  109.4 6.0 %collective-permute-start = (bf16[128,128]{1,0:T(8,128)(2,1)S(1)}, bf16[128,128]{1,0:T(8,128)(2,1)S(1)}, u32[]{:S(2)}, u32[]{:S(2)}) collective-permute-start(bf16[128,128]{1,0:T(8,128)(2,1)S(1)} %copy.67), channel_id=1, source_target_pairs={{0,1},{1,2},{2,3},{3,4},{4,5},{5,6},{6,7},{7,8},{8,9},{9,10},{10,1... | collective-permute-start | bytes 98312 | tf_op jit(solution)/shard_map/while/body/eval_jaxpr/ppermute | solution.py:12
  109.4 6.4 %collective-permute-start.1 = (bf16[128,128]{1,0:T(8,128)(2,1)S(1)}, bf16[128,128]{1,0:T(8,128)(2,1)S(1)}, u32[]{:S(2)}, u32[]{:S(2)}) collective-permute-start(bf16[128,128]{1,0:T(8,128)(2,1)S(1)} %copy.68), channel_id=1, source_target_pairs={{0,1},{1,2},{2,3},{3,4},{4,5},{5,6},{6,7},{7,8},{8,9},{9,10},{10,1... | collective-permute-start | bytes 98312 | tf_op jit(solution)/shard_map/while/body/eval_jaxpr/ppermute | solution.py:12
  111.7 6.4 %collective-permute-start.2 = (f32[128,128]{1,0:T(8,128)S(1)}, f32[128,128]{1,0:T(8,128)S(1)}, u32[]{:S(2)}, u32[]{:S(2)}) collective-permute-start(f32[128,128]{1,0:T(8,128)S(1)} %fusion.123), channel_id=1, source_target_pairs={{0,1},{1,2},{2,3},{3,4},{4,5},{5,6},{6,7},{7,8},{8,9},{9,10},{10,1... | collective-permute-start | bytes 196616 | tf_op jit(solution)/shard_map/while/body/eval_jaxpr/ppermute | solution.py:12
  112.1 6.8 %collective-permute-start.3 = (f32[128,128]{1,0:T(8,128)S(1)}, f32[128,128]{1,0:T(8,128)S(1)}, u32[]{:S(2)}, u32[]{:S(2)}) collective-permute-start(f32[128,128]{1,0:T(8,128)S(1)} %convolution_add_fusion.6), channel_id=1, source_target_pairs={{0,1},{1,2},{2,3},{3,4},{4,5},{5,6},{6,7},{7,8},{8,9},{9,10},{10,1... | collective-permute-start | bytes 196616 | tf_op jit(solution)/shard_map/while/body/eval_jaxpr/ppermute | solution.py:12
  118.9 6.0 %collective-permute-start = (bf16[128,128]{1,0:T(8,128)(2,1)S(1)}, bf16[128,128]{1,0:T(8,128)(2,1)S(1)}, u32[]{:S(2)}, u32[]{:S(2)}) collective-permute-start(bf16[128,128]{1,0:T(8,128)(2,1)S(1)} %copy.67), channel_id=1, source_target_pairs={{0,1},{1,2},{2,3},{3,4},{4,5},{5,6},{6,7},{7,8},{8,9},{9,10},{10,1... | collective-permute-start | bytes 98312 | tf_op jit(solution)/shard_map/while/body/eval_jaxpr/ppermute | solution.py:12
  118.9 6.4 %collective-permute-start.1 = (bf16[128,128]{1,0:T(8,128)(2,1)S(1)}, bf16[128,128]{1,0:T(8,128)(2,1)S(1)}, u32[]{:S(2)}, u32[]{:S(2)}) collective-permute-start(bf16[128,128]{1,0:T(8,128)(2,1)S(1)} %copy.68), channel_id=1, source_target_pairs={{0,1},{1,2},{2,3},{3,4},{4,5},{5,6},{6,7},{7,8},{8,9},{9,10},{10,1... | collective-permute-start | bytes 98312 | tf_op jit(solution)/shard_map/while/body/eval_jaxpr/ppermute | solution.py:12
  121.3 6.4 %collective-permute-start.2 = (f32[128,128]{1,0:T(8,128)S(1)}, f32[128,128]{1,0:T(8,128)S(1)}, u32[]{:S(2)}, u32[]{:S(2)}) collective-permute-start(f32[128,128]{1,0:T(8,128)S(1)} %fusion.123), channel_id=1, source_target_pairs={{0,1},{1,2},{2,3},{3,4},{4,5},{5,6},{6,7},{7,8},{8,9},{9,10},{10,1... | collective-permute-start | bytes 196616 | tf_op jit(solution)/shard_map/while/body/eval_jaxpr/ppermute | solution.py:12
  121.6 6.8 %collective-permute-start.3 = (f32[128,128]{1,0:T(8,128)S(1)}, f32[128,128]{1,0:T(8,128)S(1)}, u32[]{:S(2)}, u32[]{:S(2)}) collective-permute-start(f32[128,128]{1,0:T(8,128)S(1)} %convolution_add_fusion.6), channel_id=1, source_target_pairs={{0,1},{1,2},{2,3},{3,4},{4,5},{5,6},{6,7},{7,8},{8,9},{9,10},{10,1... | collective-permute-start | bytes 196616 | tf_op jit(solution)/shard_map/while/body/eval_jaxpr/ppermute | solution.py:12
  128.4 6.0 %collective-permute-start = (bf16[128,128]{1,0:T(8,128)(2,1)S(1)}, bf16[128,128]{1,0:T(8,128)(2,1)S(1)}, u32[]{:S(2)}, u32[]{:S(2)}) collective-permute-start(bf16[128,128]{1,0:T(8,128)(2,1)S(1)} %copy.67), channel_id=1, source_target_pairs={{0,1},{1,2},{2,3},{3,4},{4,5},{5,6},{6,7},{7,8},{8,9},{9,10},{10,1... | collective-permute-start | bytes 98312 | tf_op jit(solution)/shard_map/while/body/eval_jaxpr/ppermute | solution.py:12
  128.4 6.4 %collective-permute-start.1 = (bf16[128,128]{1,0:T(8,128)(2,1)S(1)}, bf16[128,128]{1,0:T(8,128)(2,1)S(1)}, u32[]{:S(2)}, u32[]{:S(2)}) collective-permute-start(bf16[128,128]{1,0:T(8,128)(2,1)S(1)} %copy.68), channel_id=1, source_target_pairs={{0,1},{1,2},{2,3},{3,4},{4,5},{5,6},{6,7},{7,8},{8,9},{9,10},{10,1... | collective-permute-start | bytes 98312 | tf_op jit(solution)/shard_map/while/body/eval_jaxpr/ppermute | solution.py:12
  130.8 6.4 %collective-permute-start.2 = (f32[128,128]{1,0:T(8,128)S(1)}, f32[128,128]{1,0:T(8,128)S(1)}, u32[]{:S(2)}, u32[]{:S(2)}) collective-permute-start(f32[128,128]{1,0:T(8,128)S(1)} %fusion.123), channel_id=1, source_target_pairs={{0,1},{1,2},{2,3},{3,4},{4,5},{5,6},{6,7},{7,8},{8,9},{9,10},{10,1... | collective-permute-start | bytes 196616 | tf_op jit(solution)/shard_map/while/body/eval_jaxpr/ppermute | solution.py:12
  131.1 6.8 %collective-permute-start.3 = (f32[128,128]{1,0:T(8,128)S(1)}, f32[128,128]{1,0:T(8,128)S(1)}, u32[]{:S(2)}, u32[]{:S(2)}) collective-permute-start(f32[128,128]{1,0:T(8,128)S(1)} %convolution_add_fusion.6), channel_id=1, source_target_pairs={{0,1},{1,2},{2,3},{3,4},{4,5},{5,6},{6,7},{7,8},{8,9},{9,10},{10,1... | collective-permute-start | bytes 196616 | tf_op jit(solution)/shard_map/while/body/eval_jaxpr/ppermute | solution.py:12
  138.0 6.0 %collective-permute-start = (bf16[128,128]{1,0:T(8,128)(2,1)S(1)}, bf16[128,128]{1,0:T(8,128)(2,1)S(1)}, u32[]{:S(2)}, u32[]{:S(2)}) collective-permute-start(bf16[128,128]{1,0:T(8,128)(2,1)S(1)} %copy.67), channel_id=1, source_target_pairs={{0,1},{1,2},{2,3},{3,4},{4,5},{5,6},{6,7},{7,8},{8,9},{9,10},{10,1... | collective-permute-start | bytes 98312 | tf_op jit(solution)/shard_map/while/body/eval_jaxpr/ppermute | solution.py:12
  138.0 6.4 %collective-permute-start.1 = (bf16[128,128]{1,0:T(8,128)(2,1)S(1)}, bf16[128,128]{1,0:T(8,128)(2,1)S(1)}, u32[]{:S(2)}, u32[]{:S(2)}) collective-permute-start(bf16[128,128]{1,0:T(8,128)(2,1)S(1)} %copy.68), channel_id=1, source_target_pairs={{0,1},{1,2},{2,3},{3,4},{4,5},{5,6},{6,7},{7,8},{8,9},{9,10},{10,1... | collective-permute-start | bytes 98312 | tf_op jit(solution)/shard_map/while/body/eval_jaxpr/ppermute | solution.py:12
  140.3 6.4 %collective-permute-start.2 = (f32[128,128]{1,0:T(8,128)S(1)}, f32[128,128]{1,0:T(8,128)S(1)}, u32[]{:S(2)}, u32[]{:S(2)}) collective-permute-start(f32[128,128]{1,0:T(8,128)S(1)} %fusion.123), channel_id=1, source_target_pairs={{0,1},{1,2},{2,3},{3,4},{4,5},{5,6},{6,7},{7,8},{8,9},{9,10},{10,1... | collective-permute-start | bytes 196616 | tf_op jit(solution)/shard_map/while/body/eval_jaxpr/ppermute | solution.py:12
  140.6 6.8 %collective-permute-start.3 = (f32[128,128]{1,0:T(8,128)S(1)}, f32[128,128]{1,0:T(8,128)S(1)}, u32[]{:S(2)}, u32[]{:S(2)}) collective-permute-start(f32[128,128]{1,0:T(8,128)S(1)} %convolution_add_fusion.6), channel_id=1, source_target_pairs={{0,1},{1,2},{2,3},{3,4},{4,5},{5,6},{6,7},{7,8},{8,9},{9,10},{10,1... | collective-permute-start | bytes 196616 | tf_op jit(solution)/shard_map/while/body/eval_jaxpr/ppermute | solution.py:12
  147.5 6.0 %collective-permute-start = (bf16[128,128]{1,0:T(8,128)(2,1)S(1)}, bf16[128,128]{1,0:T(8,128)(2,1)S(1)}, u32[]{:S(2)}, u32[]{:S(2)}) collective-permute-start(bf16[128,128]{1,0:T(8,128)(2,1)S(1)} %copy.67), channel_id=1, source_target_pairs={{0,1},{1,2},{2,3},{3,4},{4,5},{5,6},{6,7},{7,8},{8,9},{9,10},{10,1... | collective-permute-start | bytes 98312 | tf_op jit(solution)/shard_map/while/body/eval_jaxpr/ppermute | solution.py:12
  147.5 6.4 %collective-permute-start.1 = (bf16[128,128]{1,0:T(8,128)(2,1)S(1)}, bf16[128,128]{1,0:T(8,128)(2,1)S(1)}, u32[]{:S(2)}, u32[]{:S(2)}) collective-permute-start(bf16[128,128]{1,0:T(8,128)(2,1)S(1)} %copy.68), channel_id=1, source_target_pairs={{0,1},{1,2},{2,3},{3,4},{4,5},{5,6},{6,7},{7,8},{8,9},{9,10},{10,1... | collective-permute-start | bytes 98312 | tf_op jit(solution)/shard_map/while/body/eval_jaxpr/ppermute | solution.py:12
  149.9 6.4 %collective-permute-start.2 = (f32[128,128]{1,0:T(8,128)S(1)}, f32[128,128]{1,0:T(8,128)S(1)}, u32[]{:S(2)}, u32[]{:S(2)}) collective-permute-start(f32[128,128]{1,0:T(8,128)S(1)} %fusion.123), channel_id=1, source_target_pairs={{0,1},{1,2},{2,3},{3,4},{4,5},{5,6},{6,7},{7,8},{8,9},{9,10},{10,1... | collective-permute-start | bytes 196616 | tf_op jit(solution)/shard_map/while/body/eval_jaxpr/ppermute | solution.py:12
  150.2 6.8 %collective-permute-start.3 = (f32[128,128]{1,0:T(8,128)S(1)}, f32[128,128]{1,0:T(8,128)S(1)}, u32[]{:S(2)}, u32[]{:S(2)}) collective-permute-start(f32[128,128]{1,0:T(8,128)S(1)} %convolution_add_fusion.6), channel_id=1, source_target_pairs={{0,1},{1,2},{2,3},{3,4},{4,5},{5,6},{6,7},{7,8},{8,9},{9,10},{10,1... | collective-permute-start | bytes 196616 | tf_op jit(solution)/shard_map/while/body/eval_jaxpr/ppermute | solution.py:12
  157.0 6.0 %collective-permute-start = (bf16[128,128]{1,0:T(8,128)(2,1)S(1)}, bf16[128,128]{1,0:T(8,128)(2,1)S(1)}, u32[]{:S(2)}, u32[]{:S(2)}) collective-permute-start(bf16[128,128]{1,0:T(8,128)(2,1)S(1)} %copy.67), channel_id=1, source_target_pairs={{0,1},{1,2},{2,3},{3,4},{4,5},{5,6},{6,7},{7,8},{8,9},{9,10},{10,1... | collective-permute-start | bytes 98312 | tf_op jit(solution)/shard_map/while/body/eval_jaxpr/ppermute | solution.py:12
  157.0 6.4 %collective-permute-start.1 = (bf16[128,128]{1,0:T(8,128)(2,1)S(1)}, bf16[128,128]{1,0:T(8,128)(2,1)S(1)}, u32[]{:S(2)}, u32[]{:S(2)}) collective-permute-start(bf16[128,128]{1,0:T(8,128)(2,1)S(1)} %copy.68), channel_id=1, source_target_pairs={{0,1},{1,2},{2,3},{3,4},{4,5},{5,6},{6,7},{7,8},{8,9},{9,10},{10,1... | collective-permute-start | bytes 98312 | tf_op jit(solution)/shard_map/while/body/eval_jaxpr/ppermute | solution.py:12
  159.4 6.4 %collective-permute-start.2 = (f32[128,128]{1,0:T(8,128)S(1)}, f32[128,128]{1,0:T(8,128)S(1)}, u32[]{:S(2)}, u32[]{:S(2)}) collective-permute-start(f32[128,128]{1,0:T(8,128)S(1)} %fusion.123), channel_id=1, source_target_pairs={{0,1},{1,2},{2,3},{3,4},{4,5},{5,6},{6,7},{7,8},{8,9},{9,10},{10,1... | collective-permute-start | bytes 196616 | tf_op jit(solution)/shard_map/while/body/eval_jaxpr/ppermute | solution.py:12
  159.7 6.8 %collective-permute-start.3 = (f32[128,128]{1,0:T(8,128)S(1)}, f32[128,128]{1,0:T(8,128)S(1)}, u32[]{:S(2)}, u32[]{:S(2)}) collective-permute-start(f32[128,128]{1,0:T(8,128)S(1)} %convolution_add_fusion.6), channel_id=1, source_target_pairs={{0,1},{1,2},{2,3},{3,4},{4,5},{5,6},{6,7},{7,8},{8,9},{9,10},{10,1... | collective-permute-start | bytes 196616 | tf_op jit(solution)/shard_map/while/body/eval_jaxpr/ppermute | solution.py:12
  166.6 6.0 %collective-permute-start = (bf16[128,128]{1,0:T(8,128)(2,1)S(1)}, bf16[128,128]{1,0:T(8,128)(2,1)S(1)}, u32[]{:S(2)}, u32[]{:S(2)}) collective-permute-start(bf16[128,128]{1,0:T(8,128)(2,1)S(1)} %copy.67), channel_id=1, source_target_pairs={{0,1},{1,2},{2,3},{3,4},{4,5},{5,6},{6,7},{7,8},{8,9},{9,10},{10,1... | collective-permute-start | bytes 98312 | tf_op jit(solution)/shard_map/while/body/eval_jaxpr/ppermute | solution.py:12
  166.6 6.4 %collective-permute-start.1 = (bf16[128,128]{1,0:T(8,128)(2,1)S(1)}, bf16[128,128]{1,0:T(8,128)(2,1)S(1)}, u32[]{:S(2)}, u32[]{:S(2)}) collective-permute-start(bf16[128,128]{1,0:T(8,128)(2,1)S(1)} %copy.68), channel_id=1, source_target_pairs={{0,1},{1,2},{2,3},{3,4},{4,5},{5,6},{6,7},{7,8},{8,9},{9,10},{10,1... | collective-permute-start | bytes 98312 | tf_op jit(solution)/shard_map/while/body/eval_jaxpr/ppermute | solution.py:12
  168.9 6.4 %collective-permute-start.2 = (f32[128,128]{1,0:T(8,128)S(1)}, f32[128,128]{1,0:T(8,128)S(1)}, u32[]{:S(2)}, u32[]{:S(2)}) collective-permute-start(f32[128,128]{1,0:T(8,128)S(1)} %fusion.123), channel_id=1, source_target_pairs={{0,1},{1,2},{2,3},{3,4},{4,5},{5,6},{6,7},{7,8},{8,9},{9,10},{10,1... | collective-permute-start | bytes 196616 | tf_op jit(solution)/shard_map/while/body/eval_jaxpr/ppermute | solution.py:12
  169.2 6.8 %collective-permute-start.3 = (f32[128,128]{1,0:T(8,128)S(1)}, f32[128,128]{1,0:T(8,128)S(1)}, u32[]{:S(2)}, u32[]{:S(2)}) collective-permute-start(f32[128,128]{1,0:T(8,128)S(1)} %convolution_add_fusion.6), channel_id=1, source_target_pairs={{0,1},{1,2},{2,3},{3,4},{4,5},{5,6},{6,7},{7,8},{8,9},{9,10},{10,1... | collective-permute-start | bytes 196616 | tf_op jit(solution)/shard_map/while/body/eval_jaxpr/ppermute | solution.py:12
  176.1 6.0 %collective-permute-start = (bf16[128,128]{1,0:T(8,128)(2,1)S(1)}, bf16[128,128]{1,0:T(8,128)(2,1)S(1)}, u32[]{:S(2)}, u32[]{:S(2)}) collective-permute-start(bf16[128,128]{1,0:T(8,128)(2,1)S(1)} %copy.67), channel_id=1, source_target_pairs={{0,1},{1,2},{2,3},{3,4},{4,5},{5,6},{6,7},{7,8},{8,9},{9,10},{10,1... | collective-permute-start | bytes 98312 | tf_op jit(solution)/shard_map/while/body/eval_jaxpr/ppermute | solution.py:12
  176.1 6.4 %collective-permute-start.1 = (bf16[128,128]{1,0:T(8,128)(2,1)S(1)}, bf16[128,128]{1,0:T(8,128)(2,1)S(1)}, u32[]{:S(2)}, u32[]{:S(2)}) collective-permute-start(bf16[128,128]{1,0:T(8,128)(2,1)S(1)} %copy.68), channel_id=1, source_target_pairs={{0,1},{1,2},{2,3},{3,4},{4,5},{5,6},{6,7},{7,8},{8,9},{9,10},{10,1... | collective-permute-start | bytes 98312 | tf_op jit(solution)/shard_map/while/body/eval_jaxpr/ppermute | solution.py:12
  178.5 6.4 %collective-permute-start.2 = (f32[128,128]{1,0:T(8,128)S(1)}, f32[128,128]{1,0:T(8,128)S(1)}, u32[]{:S(2)}, u32[]{:S(2)}) collective-permute-start(f32[128,128]{1,0:T(8,128)S(1)} %fusion.123), channel_id=1, source_target_pairs={{0,1},{1,2},{2,3},{3,4},{4,5},{5,6},{6,7},{7,8},{8,9},{9,10},{10,1... | collective-permute-start | bytes 196616 | tf_op jit(solution)/shard_map/while/body/eval_jaxpr/ppermute | solution.py:12
  178.8 6.8 %collective-permute-start.3 = (f32[128,128]{1,0:T(8,128)S(1)}, f32[128,128]{1,0:T(8,128)S(1)}, u32[]{:S(2)}, u32[]{:S(2)}) collective-permute-start(f32[128,128]{1,0:T(8,128)S(1)} %convolution_add_fusion.6), channel_id=1, source_target_pairs={{0,1},{1,2},{2,3},{3,4},{4,5},{5,6},{6,7},{7,8},{8,9},{9,10},{10,1... | collective-permute-start | bytes 196616 | tf_op jit(solution)/shard_map/while/body/eval_jaxpr/ppermute | solution.py:12
  185.6 6.0 %collective-permute-start = (bf16[128,128]{1,0:T(8,128)(2,1)S(1)}, bf16[128,128]{1,0:T(8,128)(2,1)S(1)}, u32[]{:S(2)}, u32[]{:S(2)}) collective-permute-start(bf16[128,128]{1,0:T(8,128)(2,1)S(1)} %copy.67), channel_id=1, source_target_pairs={{0,1},{1,2},{2,3},{3,4},{4,5},{5,6},{6,7},{7,8},{8,9},{9,10},{10,1... | collective-permute-start | bytes 98312 | tf_op jit(solution)/shard_map/while/body/eval_jaxpr/ppermute | solution.py:12
  185.6 6.4 %collective-permute-start.1 = (bf16[128,128]{1,0:T(8,128)(2,1)S(1)}, bf16[128,128]{1,0:T(8,128)(2,1)S(1)}, u32[]{:S(2)}, u32[]{:S(2)}) collective-permute-start(bf16[128,128]{1,0:T(8,128)(2,1)S(1)} %copy.68), channel_id=1, source_target_pairs={{0,1},{1,2},{2,3},{3,4},{4,5},{5,6},{6,7},{7,8},{8,9},{9,10},{10,1... | collective-permute-start | bytes 98312 | tf_op jit(solution)/shard_map/while/body/eval_jaxpr/ppermute | solution.py:12
  188.0 6.4 %collective-permute-start.2 = (f32[128,128]{1,0:T(8,128)S(1)}, f32[128,128]{1,0:T(8,128)S(1)}, u32[]{:S(2)}, u32[]{:S(2)}) collective-permute-start(f32[128,128]{1,0:T(8,128)S(1)} %fusion.123), channel_id=1, source_target_pairs={{0,1},{1,2},{2,3},{3,4},{4,5},{5,6},{6,7},{7,8},{8,9},{9,10},{10,1... | collective-permute-start | bytes 196616 | tf_op jit(solution)/shard_map/while/body/eval_jaxpr/ppermute | solution.py:12
  188.3 6.8 %collective-permute-start.3 = (f32[128,128]{1,0:T(8,128)S(1)}, f32[128,128]{1,0:T(8,128)S(1)}, u32[]{:S(2)}, u32[]{:S(2)}) collective-permute-start(f32[128,128]{1,0:T(8,128)S(1)} %convolution_add_fusion.6), channel_id=1, source_target_pairs={{0,1},{1,2},{2,3},{3,4},{4,5},{5,6},{6,7},{7,8},{8,9},{9,10},{10,1... | collective-permute-start | bytes 196616 | tf_op jit(solution)/shard_map/while/body/eval_jaxpr/ppermute | solution.py:12
  195.2 6.0 %collective-permute-start = (bf16[128,128]{1,0:T(8,128)(2,1)S(1)}, bf16[128,128]{1,0:T(8,128)(2,1)S(1)}, u32[]{:S(2)}, u32[]{:S(2)}) collective-permute-start(bf16[128,128]{1,0:T(8,128)(2,1)S(1)} %copy.67), channel_id=1, source_target_pairs={{0,1},{1,2},{2,3},{3,4},{4,5},{5,6},{6,7},{7,8},{8,9},{9,10},{10,1... | collective-permute-start | bytes 98312 | tf_op jit(solution)/shard_map/while/body/eval_jaxpr/ppermute | solution.py:12
  195.2 6.4 %collective-permute-start.1 = (bf16[128,128]{1,0:T(8,128)(2,1)S(1)}, bf16[128,128]{1,0:T(8,128)(2,1)S(1)}, u32[]{:S(2)}, u32[]{:S(2)}) collective-permute-start(bf16[128,128]{1,0:T(8,128)(2,1)S(1)} %copy.68), channel_id=1, source_target_pairs={{0,1},{1,2},{2,3},{3,4},{4,5},{5,6},{6,7},{7,8},{8,9},{9,10},{10,1... | collective-permute-start | bytes 98312 | tf_op jit(solution)/shard_map/while/body/eval_jaxpr/ppermute | solution.py:12
  197.5 6.4 %collective-permute-start.2 = (f32[128,128]{1,0:T(8,128)S(1)}, f32[128,128]{1,0:T(8,128)S(1)}, u32[]{:S(2)}, u32[]{:S(2)}) collective-permute-start(f32[128,128]{1,0:T(8,128)S(1)} %fusion.123), channel_id=1, source_target_pairs={{0,1},{1,2},{2,3},{3,4},{4,5},{5,6},{6,7},{7,8},{8,9},{9,10},{10,1... | collective-permute-start | bytes 196616 | tf_op jit(solution)/shard_map/while/body/eval_jaxpr/ppermute | solution.py:12
  197.8 6.8 %collective-permute-start.3 = (f32[128,128]{1,0:T(8,128)S(1)}, f32[128,128]{1,0:T(8,128)S(1)}, u32[]{:S(2)}, u32[]{:S(2)}) collective-permute-start(f32[128,128]{1,0:T(8,128)S(1)} %convolution_add_fusion.6), channel_id=1, source_target_pairs={{0,1},{1,2},{2,3},{3,4},{4,5},{5,6},{6,7},{7,8},{8,9},{9,10},{10,1... | collective-permute-start | bytes 196616 | tf_op jit(solution)/shard_map/while/body/eval_jaxpr/ppermute | solution.py:12
  204.7 6.0 %collective-permute-start = (bf16[128,128]{1,0:T(8,128)(2,1)S(1)}, bf16[128,128]{1,0:T(8,128)(2,1)S(1)}, u32[]{:S(2)}, u32[]{:S(2)}) collective-permute-start(bf16[128,128]{1,0:T(8,128)(2,1)S(1)} %copy.67), channel_id=1, source_target_pairs={{0,1},{1,2},{2,3},{3,4},{4,5},{5,6},{6,7},{7,8},{8,9},{9,10},{10,1... | collective-permute-start | bytes 98312 | tf_op jit(solution)/shard_map/while/body/eval_jaxpr/ppermute | solution.py:12
  204.7 6.4 %collective-permute-start.1 = (bf16[128,128]{1,0:T(8,128)(2,1)S(1)}, bf16[128,128]{1,0:T(8,128)(2,1)S(1)}, u32[]{:S(2)}, u32[]{:S(2)}) collective-permute-start(bf16[128,128]{1,0:T(8,128)(2,1)S(1)} %copy.68), channel_id=1, source_target_pairs={{0,1},{1,2},{2,3},{3,4},{4,5},{5,6},{6,7},{7,8},{8,9},{9,10},{10,1... | collective-permute-start | bytes 98312 | tf_op jit(solution)/shard_map/while/body/eval_jaxpr/ppermute | solution.py:12
  207.1 6.4 %collective-permute-start.2 = (f32[128,128]{1,0:T(8,128)S(1)}, f32[128,128]{1,0:T(8,128)S(1)}, u32[]{:S(2)}, u32[]{:S(2)}) collective-permute-start(f32[128,128]{1,0:T(8,128)S(1)} %fusion.123), channel_id=1, source_target_pairs={{0,1},{1,2},{2,3},{3,4},{4,5},{5,6},{6,7},{7,8},{8,9},{9,10},{10,1... | collective-permute-start | bytes 196616 | tf_op jit(solution)/shard_map/while/body/eval_jaxpr/ppermute | solution.py:12
  207.4 6.8 %collective-permute-start.3 = (f32[128,128]{1,0:T(8,128)S(1)}, f32[128,128]{1,0:T(8,128)S(1)}, u32[]{:S(2)}, u32[]{:S(2)}) collective-permute-start(f32[128,128]{1,0:T(8,128)S(1)} %convolution_add_fusion.6), channel_id=1, source_target_pairs={{0,1},{1,2},{2,3},{3,4},{4,5},{5,6},{6,7},{7,8},{8,9},{9,10},{10,1... | collective-permute-start | bytes 196616 | tf_op jit(solution)/shard_map/while/body/eval_jaxpr/ppermute | solution.py:12
  214.7 6.4 %collective-permute-start.5 = (f32[128,128]{1,0:T(8,128)S(1)}, f32[128,128]{1,0:T(8,128)S(1)}, u32[]{:S(2)}, u32[]{:S(2)}) collective-permute-start(f32[128,128]{1,0:T(8,128)S(1)} %convolution_add_fusion.2), channel_id=1, source_target_pairs={{0,1},{1,2},{2,3},{3,4},{4,5},{5,6},{6,7},{7,8},{8,9},{9,10},{10,1... | collective-permute-start | bytes 196616 | tf_op jit(solution)/shard_map/ppermute | solution.py:12
  215.1 6.7 %collective-permute-start.4 = (f32[128,128]{1,0:T(8,128)S(1)}, f32[128,128]{1,0:T(8,128)S(1)}, u32[]{:S(2)}, u32[]{:S(2)}) collective-permute-start(f32[128,128]{1,0:T(8,128)S(1)} %fusion.45), channel_id=1, source_target_pairs={{0,1},{1,2},{2,3},{3,4},{4,5},{5,6},{6,7},{7,8},{8,9},{9,10},{10,1... | collective-permute-start | bytes 196616 | tf_op jit(solution)/shard_map/ppermute | solution.py:12
  (3 other events, 2.4 us)
Sparse Core Ops, SparseCore 0:
  10.8 40.6 all-gather.1
